TPU v7x, 32 devices: a whole 2x2x4 slice. The times are simulated.
32 devices in a mesh: pix: 16 (over z, x, core), ch: 2 (over y).
Axes of the slice: x: 2, y: 2, z: 4, core: 2. Of those that a mesh axis runs over, the one named last changes fastest.
Arguments:
- features: float32 [1536, 64, 256], P('pix', None, 'ch'), may hold values from -250 to 250, as said below
- sea_mask: int32 [1536, 64], P('pix'), may hold values from 0 to 1, as said below
- edge_flip: int32 [4, 2], replicated, may hold values from 0 to 1
- w_first: float32 [3, 3, 256, 256], P(None, None, None, 'ch'), may hold values from -0.125 to 0.125
- b_first: float32 [256], P('ch'), may hold values from -1.5 to 1.5
- w_second: float32 [3, 3, 256, 256], P(None, None, None, 'ch'), may hold values from -0.125 to 0.125
- b_second: float32 [256], P('ch'), may hold values from -1.5 to 1.5
- w_skip: float32 [256, 256], P(None, 'ch'), may hold values from -0.375 to 0.375
- b_skip: float32 [256], P('ch'), may hold values from -1.5 to 1.5
- run_mean: float32 [256], P('ch'), may hold values from -4 to 4
- run_var: float32 [256], P('ch'), may hold values from 0.5 to 20
- cotangent: float32 [1536, 64, 256], P('pix', None, 'ch'), may hold values from -6 to 6
Outputs:
- output: float32 [1536, 64, 256], P('pix', None, 'ch')
- grad_features: float32 [1536, 64, 256], P('pix', None, 'ch')
- grad_w_first: float32 [3, 3, 256, 256], P(None, None, None, 'ch')
- grad_b_first: float32 [256], P('ch')
- grad_w_second: float32 [3, 3, 256, 256], P(None, None, None, 'ch')
- grad_b_second: float32 [256], P('ch')
- grad_w_skip: float32 [256, 256], P(None, 'ch')
- grad_b_skip: float32 [256], P('ch')
- new_mean: float32 [256], P('ch')
- new_var: float32 [256], P('ch')
Inputs may be any that keep to these rules, and one draw needn't show every extreme that they name: `features`: channels of one field, scaled. `sea_mask`: 1 marks a valid sea pixel; the share of sea pixels is drawn for each face. `edge_flip`: entry [r, 0] reverses ribbon r's top rim, entry [r, 1] its bottom rim.
All inputs are finite; a program needn't handle non-finite values.
Results may differ from a plain program's by a relative error of at most 0.0003.
Values sent between devices are 32-bit elements; how exact they have to be, the bound alone decides.
No kernel may reach another device: no remote copies, remote signals or barrier semaphores. Data moves between devices by JAX's collectives and lax.ppermute only.
A program may use at most 256 MiB of HBM per device.

v0:
```python
import functools

import jax
import jax.numpy as jnp
from jax import lax
from jax.experimental import pallas as pl
from jax.experimental.pallas import tpu as pltpu
from jax.sharding import PartitionSpec as P

EPSILON = 1e-05
MOMENTUM = 0.1
INV_ROOT_TWO_PI = 0.3989422804014327
SQRT_HALF = 0.7071067811865476
F32 = jnp.float32
BF16 = jnp.bfloat16
VMEM_LIMIT = 60 * 1024 * 1024
LARGE = 512 * 1024


def split(value):
    high = value.astype(BF16)
    return high, (value - high.astype(F32)).astype(BF16)


def dot_split(a_high, a_low, b_high, b_low):
    total = jnp.dot(a_high, b_high, preferred_element_type=F32)
    total = total + jnp.dot(a_high, b_low, preferred_element_type=F32)
    return total + jnp.dot(a_low, b_high, preferred_element_type=F32)


def gelu_and_slope(u):
    cdf = 0.5 * (1.0 + lax.erf(u * SQRT_HALF))
    return u * cdf, cdf + u * jnp.exp(-0.5 * u * u) * INV_ROOT_TWO_PI


AT_TOP, AT_BOTTOM, SIDE, HALF, FLIPPED, PIX = range(6)
NOT_SEA = 1e30
LANES = 128


def lane_parts(depth):
    return [slice(start, start + LANES) for start in range(0, depth, LANES)]


def put_row(buffers, block, read, left, right, breadth, depth):
    high, low = buffers
    column = lax.broadcasted_iota(jnp.int32, (breadth, 1), 0)
    rows = block_rows(block, breadth)
    for lanes in lane_parts(depth):
        value = read(lanes)
        shifts = (
            jnp.where(column == 0, left(lanes), pltpu.roll(value, 1, 0)),
            value,
            jnp.where(column == breadth - 1, right(lanes), pltpu.roll(value, breadth - 1, 0)),
        )
        for tap, piece in enumerate(shifts):
            place = slice(tap * depth + lanes.start, tap * depth + lanes.stop)
            high[rows, place], low[rows, place] = split(piece)


def conv_tile(buffers, w_high, w_low, total, tile, breadth):
    high, low = buffers
    value = None
    for row_tap in range(3):
        rows = slice(row_tap * breadth, (row_tap + tile) * breadth)
        part = dot_split(high[rows, :], low[rows, :], w_high[row_tap], w_low[row_tap])
        value = part if value is None else value + part
    total[...] = value


def block_rows(block, breadth):
    start = block * breadth
    return pl.ds(start if isinstance(start, int) else pl.multiple_of(start, breadth), breadth)


def pipeline(fills, multiply, finish, tiles, tile, store=lambda tile: None, more=lambda *step: None):
    def fill(step, slot, fresh):
        for count, lay in fills:
            for block in range(count):
                lay(step, slot, block)
        more(step, slot, fresh)

    def finish_all(step, slot):
        for block in range(tile):
            finish(step, slot, block)

    for count, lay in fills:
        pl.loop(0, count)(functools.partial(lay, 0, 0))
    more(0, 0, True)

    @pl.loop(0, (tiles + 1) // 2)
    def _(step):
        now = 2 * step
        fill(jnp.minimum(now + 1, tiles - 1), 1, now + 1 < tiles)
        multiply(0)
        finish_all(jnp.maximum(now - 1, 0), 1)
        fill(jnp.minimum(now + 2, tiles - 1), 0, now + 2 < tiles)
        multiply(1)
        finish_all(now, 0)

        @pl.when(step > 0)
        def _():
            store(now - 1)

        store(now)

    if tiles % 2 == 0:
        pl.loop(0, tile)(functools.partial(finish, tiles - 1, 1))
        store(tiles - 1)


def in_turn(fills, multiply, finish, tiles, tile):
    @pl.loop(0, tiles)
    def _(step):
        for count, lay in fills:
            pl.loop(0, count)(functools.partial(lay, step, 0))
        multiply(0)
        pl.loop(0, tile)(functools.partial(finish, step, 0))


def patch(flags, x, left, right, pole, top, bottom):
    breadth = x.shape[1]

    def put(at, edge):
        @pl.when(flags[FLIPPED] == 1)
        def _():
            for column in range(breadth):
                x[at, column : column + 1] = pole[breadth - 1 - column : breadth - column]

        @pl.when(flags[FLIPPED] == 0)
        def _():
            x[at] = pole[...]

        left[at : at + 1] = 0.5 * (x[at, 0:1] + left[edge : edge + 1])
        right[at : at + 1] = 0.5 * (x[at, breadth - 1 : breadth] + right[edge : edge + 1])

    @pl.when(flags[AT_TOP] == 1)
    def _():
        put(top, top + 1)

    @pl.when(flags[AT_BOTTOM] == 1)
    def _():
        put(bottom, bottom - 1)


def put_messages(flags, x, to_prev, to_next, first_row, last_row):
    rows, breadth = x.shape[0], x.shape[1]

    @pl.loop(0, rows)
    def _(row):
        to_prev[pl.ds(row, 1)] = x[row, 0:1]
        to_next[pl.ds(row, 1)] = x[row, breadth - 1 : breadth]

    to_prev[rows : rows + breadth] = x[jnp.where(flags[AT_BOTTOM] == 1, last_row, first_row)]


def first_kernel(
    traffic, flags, marked, got, halo_mine, halo_got, w_high, w_low, biases,
    scaled, x_left, x_right, hidden, slope, to_prev, to_next,
    pole, high0, low0, high1, low1, total0, total1, *, tile
):
    blocks, breadth, depth = scaled.shape
    own = depth // 2
    extra = blocks - got.shape[0]
    tail = halo_mine.shape[0] - 8
    start = flags[HALF] * (marked.shape[0] - got.shape[0])

    def normal(value, lanes):
        source = halo_mine if lanes.start == 0 else halo_got
        mean, inverse = source[tail : tail + 1], source[tail + 1 : tail + 2]
        return jnp.where(value > 0.1 * NOT_SEA, 0.0, (value - mean) * inverse)

    traffic.wait(0, 1)
    lower, upper = slice(0, own), slice(own, depth)
    main = jnp.where(flags[HALF] == 0, extra, 0)
    outer = jnp.where(flags[HALF] == 0, 0, blocks - extra)

    @pl.loop(0, got.shape[0])
    def _(row):
        scaled[main + row, :, lower] = normal(marked[start + row], lower)
        scaled[main + row, :, upper] = normal(got[row], upper)

    for row in range(extra):
        rows = slice(row * breadth, (row + 1) * breadth)
        scaled[outer + row, :, lower] = normal(halo_mine[rows], lower)
        scaled[outer + row, :, upper] = normal(halo_got[rows], upper)

    begin = extra * breadth
    for target, count in ((x_left, blocks), (x_right, blocks), (pole, breadth)):
        rows = slice(begin, begin + count)
        target[:, lower] = normal(halo_mine[rows], lower)
        target[:, upper] = normal(halo_got[rows], upper)
        begin = begin + count

    patch(flags, scaled, x_left, x_right, pole, 3, blocks - 4)
    traffic.store(0, 0, blocks)
    traffic.wait(4, 5)
    buffers, totals = ((high0, low0), (high1, low1)), (total0, total1)

    def fill(step, slot, block):
        row = jnp.minimum(step * tile + block, blocks - 1)
        put_row(
            buffers[slot], block, lambda lanes: scaled[row, :, lanes],
            lambda lanes: x_left[pl.ds(row, 1)][:, lanes], lambda lanes: x_right[pl.ds(row, 1)][:, lanes],
            breadth, depth,
        )

    def finish(step, slot, block):
        for lanes in lane_parts(depth):
            pre = totals[slot][block_rows(block, breadth), lanes] + biases[0:1, lanes]
            value, grad = gelu_and_slope(pre)
            hidden[step * tile + block, :, lanes] = value
            slope[step * tile + block, :, lanes] = grad

    def store(step):
        traffic.store(3, step * tile, tile)
        traffic.store(4, step * tile, tile)

    pipeline(
        [(tile + 2, fill)],
        lambda slot: conv_tile(buffers[slot], w_high, w_low, totals[slot], tile, breadth),
        finish, hidden.shape[0] // tile, tile, store,
    )
    put_messages(flags, hidden, to_prev, to_next, 3, blocks - 6)


def second_kernel(
    traffic, flags, x, left_in, ahead, w_high, w_low, biases, source, s_high, s_low,
    out_own, out_send, slope,
    left, right, high0, low0, high1, low1, total0, total1, skip0, skip1, sum0, sum1, *, tile
):
    blocks, breadth, depth = x.shape
    own = depth // 2
    left[...] = left_in[...]
    right[...] = ahead[:blocks]
    traffic.wait(0)
    patch(flags, x, left, right, ahead[blocks:], 2, blocks - 3)
    traffic.wait(3, 4, 6)
    buffers, totals, skips = ((high0, low0), (high1, low1)), (total0, total1), (skip0, skip1)
    sums = (sum0, sum1)

    def fill(step, slot, block):
        row = jnp.minimum(step * tile + block, blocks - 1)
        put_row(
            buffers[slot], block, lambda lanes: x[row, :, lanes],
            lambda lanes: left[pl.ds(row, 1)][:, lanes], lambda lanes: right[pl.ds(row, 1)][:, lanes],
            breadth, depth,
        )

    def fill_skip(step, slot, block):
        row = jnp.minimum(step * tile + block + 2, source.shape[0] - 1)
        rows = block_rows(block, breadth)
        for lanes in lane_parts(depth):
            place = slice(depth + lanes.start, depth + lanes.stop)
            skips[slot][rows, lanes], skips[slot][rows, place] = split(source[row, :, lanes])

    def multiply(slot):
        conv_tile(buffers[slot], w_high, w_low, totals[slot], tile, breadth)
        skip = skips[slot]
        sums[slot][...] = dot_split(skip[:, :depth], skip[:, depth:], s_high[...], s_low[...])

    def finish(step, slot, block):
        row = step * tile + block
        rows = block_rows(block, breadth)
        for lanes in lane_parts(depth):
            pre = totals[slot][rows, lanes] + biases[1:2, lanes]
            value, grad = gelu_and_slope(pre)
            slope[row, :, lanes] = grad
            value = value + sums[slot][rows, lanes] + biases[2:3, lanes]
            if lanes.stop <= own:
                out_own[row, :, lanes] = value
            else:
                out_send[row, :, lanes.start - own : lanes.stop - own] = value

    def store(step):
        for result in range(3):
            traffic.store(result, step * tile, tile)

    pipeline([(tile + 2, fill), (tile, fill_skip)], multiply, finish, slope.shape[0] // tile, tile, store)


def edge_products(edges, w_high, w_low, slot, count):
    depth = edges.shape[0] * LANES
    total = None
    for tap in range(3):
        rows = slice(slot * depth, (slot + 1) * depth)
        pieces = [edges[part, tap : tap + count] for part in range(edges.shape[0])]
        edge_high, edge_low = split(jnp.concatenate(pieces, axis=1))
        part = dot_split(edge_high, edge_low, w_high[tap, rows], w_low[tap, rows])
        total = part if total is None else total + part
    return total


def put_rims(flags, to_next, to_prev, first_rim, last_rim, top, bottom):
    count, breadth = to_prev.shape[0], top.shape[0]
    to_prev[...] = first_rim[:count]
    to_next[:count] = last_rim[:count]
    to_next[count:] = jnp.zeros((breadth, to_next.shape[1]), F32)
    column = lax.broadcasted_iota(jnp.int32, (breadth, 1), 0)

    def put(row, at, inner):
        corner_first, corner_last = 0.5 * first_rim[at : at + 1], 0.5 * last_rim[at : at + 1]
        to_prev[inner : inner + 1] += corner_first
        to_next[inner : inner + 1] += corner_last
        row = row[...] + jnp.where(column == 0, corner_first, 0.0)
        row = row + jnp.where(column == breadth - 1, corner_last, 0.0)

        @pl.when(flags[FLIPPED] == 0)
        def _():
            to_next[count:] = row

        @pl.when(flags[FLIPPED] == 1)
        def _():
            for k in range(breadth):
                to_next[count + k : count + k + 1] = row[breadth - 1 - k : breadth - k]

    @pl.when(flags[AT_TOP] == 1)
    def _():
        put(top, 0, 1)

    @pl.when(flags[AT_BOTTOM] == 1)
    def _():
        put(bottom, count - 1, count - 2)


def back_second_kernel(
    traffic, flags, cot_mine, cot_got, slope, w_high, w_low,
    out, grad, to_next, to_prev,
    high0, low0, high1, low1, total0, total1, edge_first, edge_last, *, tile
):
    blocks, breadth, depth = slope.shape
    own = depth // 2
    traffic.wait(0, 1, 2)
    edge_first[...] = jnp.zeros_like(edge_first)
    edge_last[...] = jnp.zeros_like(edge_last)
    buffers, totals = ((high0, low0), (high1, low1)), (total0, total1)

    def fill(step, slot, block):
        row = jnp.minimum(step * tile + block, blocks - 1)
        outside = (flags[AT_TOP] == 1) & (row < 2) | (flags[AT_BOTTOM] == 1) & (row >= blocks - 2)
        inside = jnp.where(outside, 0.0, 1.0)

        def read(lanes):
            cot = cot_mine[row] if lanes.stop <= own else cot_got[row]
            value = cot * slope[row, :, lanes] * inside
            grad[row, :, lanes] = value
            edge_first[lanes.start // LANES, pl.ds(row, 1)] = value[0:1]
            edge_last[lanes.start // LANES, pl.ds(row, 1)] = value[breadth - 1 : breadth]
            return value

        put_row(buffers[slot], block, read, lambda lanes: 0.0, lambda lanes: 0.0, breadth, depth)

    def finish(step, slot, block):
        out[step * tile + block] = totals[slot][block_rows(block, breadth), :]

    traffic.wait(3, 4)
    pipeline(
        [(tile + 2, fill)],
        lambda slot: conv_tile(buffers[slot], w_high, w_low, totals[slot], tile, breadth),
        finish, out.shape[0] // tile, tile, lambda step: traffic.store(0, step * tile, tile),
    )
    traffic.store(1, 0, blocks)
    rows = blocks + 4
    first_rim = edge_products(edge_first, w_high, w_low, 2, rows)
    last_rim = edge_products(edge_last, w_high, w_low, 0, rows)
    put_rims(flags, to_next, to_prev, first_rim, last_rim, out[0], out[blocks - 3])


def back_first_kernel(
    traffic, flags, grad, cot_mine, cot_got, w_high, w_low, s_high, s_low, *rest, tile, part
):
    if part:
        before_first, before_last, before_top, out_own, out_send, to_next, to_prev = rest[:7]
    else:
        out_own, out_send, rim_first, rim_last, top = rest[:5]
    high0, low0, high1, low1, total0, total1, skip0, skip1, edge_first, edge_last, result = rest[-11:]
    count, breadth, depth = grad.shape
    own = depth // 2
    begin = part * ((count - 2) // 2)
    blocks = out_own.shape[0] + 2
    edge_first[...] = jnp.zeros_like(edge_first)
    edge_last[...] = jnp.zeros_like(edge_last)
    buffers, totals, skips = ((high0, low0), (high1, low1)), (total0, total1), (skip0, skip1)
    traffic.wait(0, 1, 2)

    def fill(step, slot, block):
        at = step * tile + block
        row = begin + at - 1
        inside = jnp.where((row >= 0) & (row < count), 1.0, 0.0)
        row = jnp.clip(row, 0, count - 1)

        def read(lanes):
            value = grad[row, :, lanes] * inside
            edge_first[lanes.start // LANES, pl.ds(at, 1)] = value[0:1]
            edge_last[lanes.start // LANES, pl.ds(at, 1)] = value[breadth - 1 : breadth]
            return value

        put_row(buffers[slot], block, read, lambda lanes: 0.0, lambda lanes: 0.0, breadth, depth)

    def fill_skip(step, slot, block):
        row = begin + step * tile + block
        inside = jnp.where((row >= 1) & (row < count - 1), 1.0, 0.0)
        row = jnp.clip(row + 1, 0, cot_mine.shape[0] - 1)
        rows = block_rows(block, breadth)
        for lanes in lane_parts(depth):
            cot = cot_mine[row] if lanes.stop <= own else cot_got[row]
            place = slice(depth + lanes.start, depth + lanes.stop)
            skips[slot][rows, lanes], skips[slot][rows, place] = split(cot * inside)

    def multiply(slot):
        conv_tile(buffers[slot], w_high, w_low, totals[slot], tile, breadth)
        skip = skips[slot]
        totals[slot][...] += dot_split(skip[:, :depth], skip[:, depth:], s_high[...], s_low[...])

    def finish(step, slot, block):
        result[step * tile + block] = totals[slot][block_rows(block, breadth), :]

    traffic.wait(3, 4)
    in_turn([(tile + 2, fill), (tile, fill_skip)], multiply, finish, result.shape[0] // tile, tile)

    @pl.loop(0, out_own.shape[0])
    def _(row):
        out_own[row] = result[row + 1, :, :own]
        out_send[row] = result[row + 1, :, own:]

    traffic.store(0 if part == 0 else 0, 0, out_own.shape[0])
    traffic.store(1, 0, out_own.shape[0])
    rows = blocks + 6
    first_rim = edge_products(edge_first, w_high, w_low, 2, rows)
    last_rim = edge_products(edge_last, w_high, w_low, 0, rows)
    if part == 0:
        rim_first[...], rim_last[...] = first_rim, last_rim
        top[...] = result[0]
    else:
        joined = [
            jnp.concatenate([before[: begin + 1], now[1 : begin + 2]], axis=0)
            for before, now in ((before_first, first_rim), (before_last, last_rim))
        ]
        put_rims(flags, to_next, to_prev, *joined, before_top[...], result[blocks - 1])


def weight_kernel(traffic, flags, x, *rest, tile, first):
    if first:
        left, right, upper, behind, after, slope, cot_mine, cot_got = rest[:8]
        parts, _, total, total_skip, grad_out = rest[8:13]
        rest, begin = rest[13:], 3
    else:
        left_in, ahead, grad = rest[:3]
        parts, _, total = rest[3:6]
        left, right = rest[-2:]
        rest, begin = rest[6:-2], 2
    high0, low0, high1, low1, t0, t1, acc = rest[:7]
    buffers, turned = ((high0, low0), (high1, low1)), (t0, t1)
    breadth, depth = x.shape[1:]
    own = depth // 2
    taps = acc.shape[0]
    rows = x.shape[0] - 2 * begin - 2
    pixels = tile * breadth
    traffic.wait(0)
    if first:
        count = rows + 2
        column = lax.broadcasted_iota(jnp.int32, (breadth, 1), 0)
        traffic.wait(3, 6, 7, 8)
        total_skip[...] = jnp.zeros_like(total_skip)

        def read(row, lanes):
            at = row + 1
            edge = (flags[AT_TOP] == 1) & (row == 0) | (flags[AT_BOTTOM] == 1) & (row == rows - 1)
            value = upper[at, :, lanes] + jnp.where(column == 0, behind[pl.ds(at, 1)][:, lanes], 0.0)
            value = value + jnp.where(column == breadth - 1, after[pl.ds(at, 1)][:, lanes], 0.0)
            value = value + behind[count : count + breadth, lanes] * jnp.where(edge, 1.0, 0.0)
            value = value * slope[at + 2, :, lanes]
            grad_out[at, :, lanes] = value
            return value

        for row, pole in ((-1, AT_TOP), (rows, AT_BOTTOM)):
            for lanes in lane_parts(depth):
                value = read(row, lanes)
                grad_out[row + 1, :, lanes] = value * jnp.where(flags[pole] == 1, 0.0, 1.0)
    else:
        left[...] = left_in[...]
        right[...] = ahead[: x.shape[0]]
        patch(flags, x, left, right, ahead[x.shape[0] :], 2, x.shape[0] - 3)
        traffic.wait(3)

        def read(row, lanes):
            return grad[row + 2, :, lanes]

    acc[...] = jnp.zeros_like(acc)
    total[...] = jnp.zeros_like(total)

    def turn(slot, place, lanes, value):
        value_high, value_low = split(value.T)
        turned[slot][place, lanes] = value_high
        turned[slot][place + 1, lanes] = value_low

    def fill(step, slot, block):
        row = step * tile + block + begin
        put_row(
            buffers[slot], block, lambda lanes: x[row, :, lanes],
            lambda lanes: left[pl.ds(row, 1)][:, lanes], lambda lanes: right[pl.ds(row, 1)][:, lanes],
            breadth, depth,
        )

    def fill_turned(step, slot, fresh):
        once = jnp.where(fresh, 1.0, 0.0)
        for lanes in lane_parts(depth):
            value = jnp.concatenate([read(step * tile + block, lanes) for block in range(tile)], axis=0)
            total[:, lanes] += jnp.sum(value, axis=0, keepdims=True) * once
            turn(slot, 0, lanes, value)
            if first:
                source = cot_mine if lanes.stop <= own else cot_got
                value = source[pl.ds(step * tile + 2, tile)].reshape(pixels, LANES)
                total_skip[:, lanes] += jnp.sum(value, axis=0, keepdims=True) * once
                turn(slot, 2, lanes, value)

    def multiply(slot):
        high, low = buffers[slot]
        for tap in range(taps):
            row_tap, column_tap, place = (tap // 3, tap % 3, 0) if tap < 9 else (1, 1, 2)
            window = slice(row_tap * breadth, row_tap * breadth + pixels)
            lanes = slice(column_tap * depth, (column_tap + 1) * depth)
            acc[tap] += dot_split(
                turned[slot][place], turned[slot][place + 1], high[window, lanes], low[window, lanes]
            )

    pipeline([(tile + 2, fill)], multiply, lambda *block: None, rows // tile, 0, more=fill_turned)
    half = depth // 2
    mine = (flags[SIDE] ^ flags[PIX]) & 1
    for tap in range(taps):
        value = acc[tap].T
        parts[mine, tap] = value[:half]
        parts[1 - mine, tap] = value[half:]


def weights_kernel(traffic, flags, mine, *rest, steps, skip):
    shares, rest = rest[: steps + 1], rest[steps + 1 :]
    if skip:
        mine_skip, f_high, f_low, b_high, b_low, s_high, s_low, sb_high, sb_low, other = rest
    else:
        f_high, f_low, b_high, b_low, other = rest
    own = mine.shape[1]
    depth = 2 * own
    taps = mine.shape[0]
    count = 1 << steps
    traffic.wait(*traffic.ins)
    share, share_skip = taps // count, depth // count
    unit = shares[0].shape[0]
    begin = share if skip else 0
    for piece in range(count):
        away = sum(1 << (steps - 1 - step) for step in range(steps) if piece >> step & 1)
        index = (flags[PIX] & (count - 1)) ^ away
        level = piece.bit_length()
        source = shares[level]
        at = (piece - (1 << (level - 1)) if level else 0) * unit + begin
        other[pl.ds(pl.multiple_of(index * share, 8), share)] = source[at : at + share]
        if skip:
            start = pl.multiple_of(taps + index * share_skip, 8)
            other[pl.ds(start, share_skip)] = source[at + share : at + share + share_skip]
    def both(first, second):
        return jnp.concatenate([first, second], axis=1)

    def one_tap(row_tap, column_tap):
        tap, back_row, back_column = row_tap * 3 + column_tap, 2 - row_tap, 2 - column_tap
        for part in range(2):
            at = pl.multiple_of(tap * depth + jnp.where(flags[SIDE] == part, 0, own), own)
            value = both(mine[pl.ds(at, own)], other[pl.ds(at, own)])
            value_high, value_low = split(value)
            place = pl.ds(pl.multiple_of(column_tap * depth + part * own, own), own)
            f_high[row_tap, place] = value_high
            f_low[row_tap, place] = value_low
            turned_high, turned_low = split(value.T)
            place = pl.ds(pl.multiple_of(back_column * depth, depth), depth)
            lanes = slice(part * own, (part + 1) * own)
            b_high[back_row, place, lanes] = turned_high
            b_low[back_row, place, lanes] = turned_low

    for row_tap in range(3):
        pl.loop(0, 3)(functools.partial(one_tap, row_tap))
        for result in range(4):
            traffic.store(result, row_tap if result < 2 else 2 - row_tap, 1)

    if skip:
        for part in range(2):
            at = pl.multiple_of(jnp.where(flags[SIDE] == part, 0, own), own)
            value = both(mine_skip[pl.ds(at, own)], other[pl.ds(pl.multiple_of(taps + at, own), own)])
            lanes = slice(part * own, (part + 1) * own)
            s_high[lanes], s_low[lanes] = split(value)
            sb_high[:, lanes], sb_low[:, lanes] = split(value.T)


def pre_kernel(traffic, flags, features, mask, marked, theirs, stats, inner, to_prev, to_next):
    rows, breadth, own = features.shape
    length = theirs.shape[0]
    traffic.wait(0)
    start = (1 - flags[HALF]) * (rows - length)
    turned = mask[...].astype(F32)
    turned = jnp.concatenate([turned, jnp.zeros((breadth, 128 - rows), F32)], axis=1)
    none = jnp.zeros((8, own), F32)

    def fold(v):
        return jnp.sum(v.reshape(breadth // 8, 8, own), axis=0)

    def first(step, carry):
        count, total = carry
        base = step * 8
        sea_of = pltpu.roll(turned, 128 - base, 1)
        for k in range(8):
            row = base + k
            sea = jnp.broadcast_to(sea_of[:, k : k + 1], (breadth, own))
            value = features[row]
            land = jnp.where(sea > 0.5, value, NOT_SEA)
            marked[row] = land
            to_prev[pl.ds(row, 1)] = land[0:1]
            to_next[pl.ds(row, 1)] = land[breadth - 1 : breadth]
            count, total = count + fold(sea), total + fold(value * sea)
        return count, total

    count, total = lax.fori_loop(0, rows // 8, first, (none, none))
    count = jnp.sum(count, axis=0, keepdims=True)
    mean = jnp.sum(total, axis=0, keepdims=True) / jnp.maximum(count, 1.0)

    def second(step, squares):
        for k in range(8):
            value = marked[step * 8 + k]
            value = jnp.where(value > 0.1 * NOT_SEA, 0.0, value - mean)
            squares = squares + fold(value * value)
        return squares

    @pl.loop(0, length // 4)
    def _(step):
        theirs[pl.ds(step * 4, 4)] = marked[pl.ds(start + step * 4, 4)]

    traffic.store(1, 0, length)
    traffic.store(0, 0, rows)
    squares = lax.fori_loop(0, rows // 8, second, none)

    stats[...] = jnp.zeros_like(stats)
    stats[0:1] = count
    stats[1:2] = mean
    stats[2:3] = jnp.sum(squares, axis=0, keepdims=True)
    strip = flags[SIDE] ^ flags[HALF]
    to_prev[rows:] = marked[strip * (rows - 1)]
    inner[...] = marked[pl.ds((1 - strip) * (rows - inner.shape[0]), inner.shape[0])]


def cot_kernel(traffic, flags, cot, extra, mine, early, late):
    rows, more, count = cot.shape[0], extra.shape[0], mine.shape[0]
    traffic.wait(0)

    def put(target, begin, half):
        length = target.shape[0]

        @pl.loop(0, length)
        def _(row):
            target[row] = cot[jnp.clip(begin + row - more + half * (rows // 2), 0, rows - 1)]

        if begin == 0:

            @pl.when(half == 0)
            def _():
                target[:more] = extra[...]

        if begin + length == count:

            @pl.when(half == 1)
            def _():
                target[length - more :] = extra[...]

    put(early, 0, 1 - flags[HALF])
    put(late, early.shape[0], 1 - flags[HALF])
    put(mine, 0, flags[HALF])


def rims_kernel(traffic, flags, behind, ahead, core, stats, mine, theirs, wide):
    rows, own = behind.shape
    breadth = ahead.shape[0] - rows
    extra = (core.shape[0]) // (breadth + 2)
    length = rows // 2 + 2 * extra
    inner = extra * breadth
    at = inner
    for target in (mine, theirs):
        target[:inner] = core[:inner]
    for source, start in ((behind, inner + extra), (ahead, inner)):
        wide[:extra] = core[start : start + extra]
        wide[extra : extra + rows] = source[:rows]
        wide[extra + rows :] = core[start : start + extra]
        for target, half in ((mine, flags[HALF]), (theirs, 1 - flags[HALF])):
            target[at : at + length] = wide[pl.ds(pl.multiple_of(half * (rows // 2), 8), length)]
        at = at + length
    count, mean, squares = stats[0:1], stats[1:2], stats[2:3]
    inverse = lax.rsqrt(squares / count + EPSILON)
    for target in (mine, theirs):
        target[at : at + breadth] = ahead[rows:]
        target[at + breadth :] = jnp.zeros((8, own), F32)
        target[at + breadth : at + breadth + 1] = mean
        target[at + breadth + 1 : at + breadth + 2] = inverse


def gather_kernel(flags, second_mine, second_other, first_mine, first_other, second, first, skip, sems):
    half = second_mine.shape[1]
    here = (flags[PIX] & 1) * half
    copies = []
    for place, (mine, start) in enumerate(
        (
            (second_mine, here), (second_other, half - here),
            (first_mine, here), (first_other, half - here),
        )
    ):
        rows = pl.ds(pl.multiple_of(start, half), half)
        target = second if place < 2 else first
        copies.append(pltpu.make_async_copy(mine.at[pl.ds(0, 9)], target.at[:, rows], sems.at[place]))
        if place >= 2:
            copies.append(pltpu.make_async_copy(mine.at[9], skip.at[rows], sems.at[place + 2]))
    for copy in copies:
        copy.start()
    for copy in copies:
        copy.wait()


def gather_call(flags, *operands):
    anywhere, whole = pl.BlockSpec(memory_space=pl.ANY), pl.BlockSpec(memory_space=pltpu.VMEM)
    half, own = operands[0].shape[1:]
    shapes = [(9, 2 * half, own), (9, 2 * half, own), (2 * half, own)]
    return pl.pallas_call(
        gather_kernel,
        out_shape=[jax.ShapeDtypeStruct(shape, F32) for shape in shapes],
        in_specs=[pl.BlockSpec(memory_space=pltpu.SMEM)] + [whole] * 4,
        out_specs=[anywhere] * 3,
        scratch_shapes=[pltpu.SemaphoreType.DMA((6,))],
        compiler_params=pltpu.CompilerParams(vmem_limit_bytes=VMEM_LIMIT),
        cost_estimate=pl.CostEstimate(flops=0, bytes_accessed=12_000_000, transcendentals=0),
        name="gather",
    )(flags, *operands)


def final_kernel(flags, marked, lower_upper, lower_lower, rims, stats, sums, *rest, other, parts):
    out, source, result, in_sems, out_sems = rest[-5:]
    rows, breadth, own = marked.shape
    size = rows // 2
    step = size // parts
    last = size + 2 + breadth
    count, mean = stats[0:1], stats[1:2]
    inverse = lax.rsqrt(stats[2:3] / count + EPSILON)
    first_mean, second_mean = sums[3:4] / count, sums[4:5] / count
    column = lax.broadcasted_iota(jnp.int32, (breadth, 1), 0)
    strip = flags[SIDE] ^ flags[HALF]
    edge = strip * (size - 1)
    half = 1 - flags[HALF] if other else flags[HALF]
    at_pole = flags[SIDE] == (1 if other else 0)

    def fetch(part):
        rows = pl.ds(half * size + part * step, step)
        return pltpu.make_async_copy(marked.at[rows], source.at[pl.ds(part * step, step)], in_sems.at[part])

    def store(part):
        rows = pl.ds(half * size + part * step, step)
        return pltpu.make_async_copy(result.at[pl.ds(part * step, step)], out.at[rows], out_sems.at[part])

    for part in range(parts):
        fetch(part).start()
    for part in range(parts):
        fetch(part).wait()

        lower = lower_upper if part < parts // 2 else lower_lower

        @pl.loop(part * step, (part + 1) * step)
        def _(row):
            value = lower[row % (size // 2)] + jnp.where(column == 0, rims[pl.ds(row + 1, 1)], 0.0)
            value = value + jnp.where(column == breadth - 1, rims[pl.ds(row + last + 1, 1)], 0.0)
            at_edge = jnp.where((row == edge) & at_pole, 1.0, 0.0)
            value = value + rims[size + 2 : last] * at_edge
            normed = (source[row] - mean) * inverse
            value = inverse * (value - first_mean - normed * second_mean)
            result[row] = jnp.where(source[row] > 0.1 * NOT_SEA, 0.0, value)

        store(part).start()
    for part in range(parts):
        store(part).wait()


def final_call(other, flags, marked, lower, rims, stats, sums, before=None):
    anywhere, whole = pl.BlockSpec(memory_space=pl.ANY), pl.BlockSpec(memory_space=pltpu.VMEM)
    parts = 4
    operands = [flags, marked, *lower, rims, stats, sums] + ([before] if other else [])
    half = pltpu.VMEM((marked.shape[0] // 2,) + marked.shape[1:], F32)
    return pl.pallas_call(
        functools.partial(final_kernel, other=other, parts=parts),
        out_shape=jax.ShapeDtypeStruct(marked.shape, F32),
        in_specs=[pl.BlockSpec(memory_space=pltpu.SMEM), anywhere] + [whole] * 5 + [anywhere] * other,
        out_specs=anywhere,
        scratch_shapes=[half, half, pltpu.SemaphoreType.DMA((parts,)), pltpu.SemaphoreType.DMA((parts,))],
        input_output_aliases={7: 0} if other else {},
        compiler_params=pltpu.CompilerParams(vmem_limit_bytes=VMEM_LIMIT),
        cost_estimate=pl.CostEstimate(flops=0, bytes_accessed=4 * marked.size * 3, transcendentals=0),
        name="final_got" if other else "final_own",
    )(*operands)


def join_kernel(flags, mine, theirs, out, sems):
    size = out.shape[0] // 2
    skip = (mine.shape[0] - size) // 2
    copies = []
    for place, source in enumerate((mine, theirs)):
        half = flags[HALF] if place == 0 else 1 - flags[HALF]
        target = out.at[pl.ds(half * size, size)]
        copies.append(pltpu.make_async_copy(source.at[pl.ds(skip, size)], target, sems.at[place]))
    for copy in copies:
        copy.start()
    for copy in copies:
        copy.wait()


def call_copy(kernel, shape, flags, *operands):
    anywhere = pl.BlockSpec(memory_space=pl.ANY)
    return pl.pallas_call(
        kernel,
        out_shape=[jax.ShapeDtypeStruct(shape, F32)],
        in_specs=[pl.BlockSpec(memory_space=pltpu.SMEM)]
        + [pl.BlockSpec(memory_space=pltpu.VMEM)] * len(operands),
        out_specs=[anywhere],
        scratch_shapes=[pltpu.SemaphoreType.DMA((len(operands),))],
        compiler_params=pltpu.CompilerParams(vmem_limit_bytes=VMEM_LIMIT),
        cost_estimate=pl.CostEstimate(flops=0, bytes_accessed=0, transcendentals=0),
        name="join",
    )(flags, *operands)


class Traffic:
    def __init__(self, ins, outs):
        self.ins, self.outs, self.parts = ins, outs, {}
        for copies in ins.values():
            for copy in copies:
                copy.start()

    def wait(self, *places):
        for place in places:
            for copy in self.ins.pop(place):
                copy.wait()

    def store(self, place, start, count):
        source, target, sem = self.outs[place]
        rows = pl.ds(start, count)
        pltpu.make_async_copy(source.at[rows], target.at[rows], sem).start()
        self.parts[place] = True

    def finish(self):
        for place in self.outs:
            if place not in self.parts:
                pltpu.make_async_copy(*self.outs[place]).start()
        for place in self.outs:
            pltpu.make_async_copy(*self.outs[place]).wait()


def call(kernel, shapes, scratch, flags, *operands, name=None, paired=False):
    shapes = [s if isinstance(s, jax.ShapeDtypeStruct) else jax.ShapeDtypeStruct(s, F32) for s in shapes]

    operands = [operand if isinstance(operand, tuple) else (operand,) for operand in operands]
    wholes = [
        jax.ShapeDtypeStruct((sum(part.shape[0] for part in parts),) + parts[0].shape[1:], parts[0].dtype)
        for parts in operands
    ]
    counts = [len(parts) for parts in operands]
    operands = [part for parts in operands for part in parts]

    def large(a):
        return a.size * a.dtype.itemsize >= LARGE

    inside, outside = [large(a) for a in wholes], [large(a) for a in shapes]
    split_up = [is_large for is_large, count in zip(inside, counts) for _ in range(count)]
    buffers = [pltpu.VMEM(a.shape, a.dtype) for a in wholes + shapes[2 * paired :] if large(a)]
    if paired:
        buffers.append(pltpu.VMEM((2,) + shapes[0].shape, F32))
    sems = [pltpu.SemaphoreType.DMA((max(1, sum(group)),)) for group in (split_up, outside)]
    anywhere, whole = pl.BlockSpec(memory_space=pl.ANY), pl.BlockSpec(memory_space=pltpu.VMEM)

    def body(flags, *refs):
        refs = list(refs)
        given = len(operands) + len(shapes)
        rest, (in_sems, out_sems) = refs[given : len(refs) - 2], refs[-2:]
        held, extra = rest[: len(buffers)], rest[len(buffers) :]
        ins, outs, seen, sources, started = {}, {}, [], refs[: len(operands)], 0
        for place, is_large in enumerate(inside):
            parts = [sources.pop(0) for _ in range(counts[place])]
            if not is_large:
                seen.append(parts[0])
                continue
            buffer, row = held.pop(0), 0
            ins[place] = []
            for part in parts:
                target = buffer.at[pl.ds(row, part.shape[0])] if len(parts) > 1 else buffer
                ins[place].append(pltpu.make_async_copy(part, target, in_sems.at[started]))
                row, started = row + part.shape[0], started + 1
            seen.append(buffer)
        for place, is_large in enumerate(outside):
            ref = refs[len(operands) + place]
            if paired and place < 2:
                outs[place] = (held[-1].at[place], ref, out_sems.at[len(outs)])
                seen.append(held[-1])
            elif is_large:
                buffer = held.pop(0)
                outs[place] = (buffer, ref, out_sems.at[len(outs)])
                seen.append(buffer)
            else:
                seen.append(ref)
        traffic = Traffic(ins, outs)
        kernel(traffic, flags, *seen, *extra)
        assert not traffic.ins
        traffic.finish()

    return pl.pallas_call(
        body,
        out_shape=shapes,
        in_specs=[pl.BlockSpec(memory_space=pltpu.SMEM)] + [anywhere if k else whole for k in split_up],
        out_specs=[anywhere if k else whole for k in outside],
        scratch_shapes=buffers + list(scratch) + sems,
        compiler_params=pltpu.CompilerParams(vmem_limit_bytes=VMEM_LIMIT),
        cost_estimate=pl.CostEstimate(flops=0, bytes_accessed=0, transcendentals=0),
        name=name,
    )(flags, *operands)


class Place:
    def __init__(self, mesh, rows, breadth):
        self.count = mesh.shape["pix"]
        self.strips = 3 * breadth // rows
        assert mesh.shape["ch"] == 2 and self.strips == 2
        self.pix = lax.axis_index("pix")
        self.side = lax.axis_index("ch")
        self.ribbon = self.pix // self.strips % 4
        self.strip = self.pix % self.strips
        self.half = self.side ^ self.strip
        self.at_top = (self.side == 0) & (self.strip == 0)
        self.at_bottom = (self.side == 0) & (self.strip == 1)

    def ribbon_pairs(self, offset):
        pairs = []
        for index in range(self.count):
            sample, strip = index // (4 * self.strips), index % self.strips
            ribbon = (index // self.strips + offset) % 4
            pairs.append((index, (sample * 4 + ribbon) * self.strips + strip))
        return pairs

    def to_next(self, value):
        return lax.ppermute(value, "pix", self.ribbon_pairs(1))

    def to_prev(self, value):
        return lax.ppermute(value, "pix", self.ribbon_pairs(-1))

    def across(self, value):
        return lax.ppermute(value, "ch", [(0, 1), (1, 0)])

    def flip(self, value, bit):
        return lax.ppermute(value, "pix", [(i, i ^ bit) for i in range(self.count)])

    def bits(self):
        return [1 << step for step in range(self.count.bit_length() - 1)]

    def ordered(self, mine, theirs, bit):
        upper = (self.pix & bit) != 0
        return jnp.where(upper, theirs, mine), jnp.where(upper, mine, theirs)

    def near(self):
        return self.bits()[:3]

    def members(self, bits):
        out = []
        for other in range(1, 1 << len(bits)):
            mask = sum(bit for step, bit in enumerate(bits) if other >> step & 1)
            out.append((other, [(i, i ^ mask) for i in range(self.count)]))
        return out

    def number(self, bits):
        total = 0
        for step, bit in enumerate(bits):
            total = total + (((self.pix & bit) != 0).astype(jnp.int32) << step)
        return total

    def shared(self, values, bits):
        me, length = self.number(bits), values[0].shape[0] >> len(bits)

        def share(number):
            pieces = [lax.dynamic_slice_in_dim(value, number * length, length, 0) for value in values]
            return functools.reduce(jnp.add, pieces)

        total = share(me)
        parts = []
        for other, pairs in self.members(bits):
            piece = share(me ^ other)
            parts.append(lax.ppermute(piece, "pix", pairs))
        for part in parts:
            total = total + part
        return total

    def spread(self, value, bits):
        parts = [value] + [lax.ppermute(value, "pix", pairs) for _, pairs in self.members(bits)]
        for step, bit in enumerate(bits):
            upper = (self.pix & bit) != 0
            parts = [
                jnp.where(upper, parts[k ^ (1 << step)], parts[k]) for k in range(len(parts))
            ]
        return jnp.concatenate(parts, axis=0)

    def groups(self):
        bits = self.bits()
        rest = [bits[k : k + 2] for k in range(2, len(bits), 2)]
        return [bits[:1], bits[1:2]] + rest

    def summed(self, value):
        for bit in self.bits():
            first, second = self.ordered(value, self.flip(value, bit), bit)
            value = first + second
        return value

    def part(self, value, half, start, length):
        return lax.dynamic_slice_in_dim(value, half * start, length, 0)

    def join_rows(self, mine, theirs):
        return jnp.where(
            self.half == 0,
            jnp.concatenate([mine, theirs], axis=0),
            jnp.concatenate([theirs, mine], axis=0),
        )

    def inner_rows(self, value, extra):
        edge = jnp.where(self.strip == 0, value[-extra:], value[:extra])
        return self.flip(edge, 1)


def merged_stats(place, state):
    for bit in place.bits():
        first, second = place.ordered(state, place.flip(state, bit), bit)
        total = first[0] + second[0]
        safe = jnp.maximum(total, 1.0)
        step = second[1] - first[1]
        state = jnp.stack(
            [
                total,
                (first[0] * first[1] + second[0] * second[1]) / safe,
                first[2] + second[2] + step * step * (first[0] * second[0] / safe),
            ]
            + [total] * 5
        )
    return state


def local(
    mesh, features, sea_mask, edge_flip, w_first, b_first, w_second, b_second, w_skip, b_skip,
    run_mean, run_var, cotangent,
):
    rows, breadth, own = features.shape
    place = Place(mesh, rows, breadth)
    size, depth = rows // 2, 2 * own
    taps = 9 * depth
    flip_row = jnp.sum(jnp.where((jnp.arange(4) == place.ribbon)[:, None], edge_flip, 0), axis=0)
    flipped = jnp.where(place.strip == 0, flip_row[0], flip_row[1]) == 1
    flags = jnp.stack(
        [
            jnp.where(flag, 1, 0).astype(jnp.int32)
            for flag in (place.at_top, place.at_bottom, place.side == 1, place.half == 1, flipped)
        ]
        + [place.pix.astype(jnp.int32)]
    )

    w_first, w_second = w_first.reshape(taps, own), w_second.reshape(taps, own)
    near = len(place.near())
    share, share_skip, number = taps >> near, depth >> near, place.number(place.near())
    biases = jnp.stack([b_first, b_second, b_skip])
    message = jnp.concatenate(
        [
            lax.dynamic_slice_in_dim(w_first, number * share, share, 0),
            lax.dynamic_slice_in_dim(w_second, number * share, share, 0),
            lax.dynamic_slice_in_dim(w_skip, number * share_skip, share_skip, 0),
            jnp.pad(biases, ((0, 5), (0, 0))),
        ]
    )
    features, message = lax.optimization_barrier((features, message))
    message = place.across(message)
    marked, theirs, stats, inner, to_prev, to_next = call(
        pre_kernel,
        [
            (rows, breadth, own), (size + 4, breadth, own), (8, own), (4, breadth, own),
            (rows + breadth, own), (rows, own),
        ],
        [], flags, features, sea_mask.T, name="pre",
    )
    theirs, message = lax.optimization_barrier((theirs, message))
    got = place.across(theirs)
    biases = jnp.concatenate([biases, message[2 * share + share_skip :][:3]], axis=1)
    cot_inner = place.inner_rows(cotangent, 2)

    def neighbours(stats, inner, to_prev, to_next, message):
        mine = message[: 2 * share + share_skip]
        bits = place.near()
        ahead, behind = place.to_prev(to_prev), place.to_next(to_next)
        shares = [mine, place.flip(mine, bits[2])]
        shares[1], ahead, behind = lax.optimization_barrier((shares[1], ahead, behind))
        shares.append(place.flip(jnp.concatenate(shares, axis=0), bits[1]))

        def inner_part(value):
            return jnp.where(place.strip == 0, value[rows - 4 : rows], value[:4])

        core = jnp.concatenate(
            [inner.reshape(-1, own), inner_part(ahead), inner_part(behind)], axis=0
        )
        core = place.flip(core, 1)
        stats = merged_stats(place, stats)
        halo_mine, halo_theirs = call(
            rims_kernel, [(rim_rows, own)] * 2, [pltpu.VMEM((rows + 8, own), F32)],
            flags, behind, ahead, core, stats, name="rims",
        )
        late = size // 6
        cot_mine, cot_early, cot_late = call(
            cot_kernel, [(size + 4, breadth, own), (size + 4 - late, breadth, own), (late, breadth, own)],
            [], flags, cotangent, cot_inner, name="cot",
        )
        gate = (shares[2], halo_theirs, cot_early)
        shares[2], halo_theirs, cot_early = lax.optimization_barrier(gate)
        halo_got = place.across(halo_theirs)
        shares.append(place.flip(jnp.concatenate(shares, axis=0), bits[0]))
        first_weights = call(
            functools.partial(weights_kernel, steps=near, skip=False),
            kinds, [pltpu.VMEM((taps, own), F32)], flags, w_first, *shares,
            name="weights_first",
        )
        return stats, halo_mine, halo_got, cot_mine, cot_early, cot_late, shares, first_weights

    def block(steps, *operands):
        shapes = jax.eval_shape(steps, *operands)

        def nothing(*operands):
            return jax.tree.map(lambda leaf: jnp.zeros(leaf.shape, leaf.dtype), shapes)

        return lax.cond(edge_flip[0, 0] < 2, steps, nothing, *operands)

    rim_rows = 4 * breadth + 2 * (size + 8) + breadth + 8
    kinds = [jax.ShapeDtypeStruct((3, 3 * depth, depth), BF16)] * 4
    stats, halo_mine, halo_got, cot_mine, cot_early, cot_late, shares, first_weights = block(
        neighbours, stats, inner, to_prev, to_next, message
    )
    sea_count, batch_mean = stats[0], stats[1]
    batch_var = stats[2] / sea_count
    cot_early, got = lax.optimization_barrier((cot_early, got))
    cot_got = place.across(cot_early)

    small = [jax.ShapeDtypeStruct((depth, depth), BF16)] * 4
    second_weights = call(
        functools.partial(weights_kernel, steps=near, skip=True),
        kinds + small, [pltpu.VMEM((taps + depth, own), F32)], flags,
        w_second, *shares, w_skip,
        name="weights_second",
    )

    def buffers(tile):
        return [pltpu.VMEM(((tile + 2) * breadth, 3 * depth), BF16) for _ in range(4)]

    def pair(count, width, kind=F32):
        return [pltpu.VMEM((count, width), kind) for _ in range(2)]

    def edges(count):
        return [pltpu.VMEM((depth // LANES, count, LANES), F32) for _ in range(2)]

    def conv_scratch(tile):
        return buffers(tile) + pair(tile * breadth, depth)

    def first_conv(got, halo_got):
        return call(
            functools.partial(first_kernel, tile=3),
            [
                (size + 8, breadth, depth), (size + 8, depth), (size + 8, depth),
                (size + 6, breadth, depth), (size + 6, breadth, depth),
                (size + 6 + breadth, depth), (size + 6, depth),
            ],
            [pltpu.VMEM((breadth, depth), F32)] + conv_scratch(3),
            flags, marked, got, halo_mine, halo_got, *first_weights[:2], biases,
            name="first",
        )

    scaled, x_left, x_right, hidden, slope_first, to_prev, to_next = block(first_conv, got, halo_got)
    h_ahead, h_left = place.to_prev(to_prev), place.to_next(to_next)
    h_left, cot_got = lax.optimization_barrier((h_left, cot_got))
    cot_got = (cot_got, place.across(cot_late))
    out_own, out_send, slope_second = call(
        functools.partial(second_kernel, tile=4),
        [(size + 4, breadth, own), (size + 4, breadth, own), (size + 4, breadth, depth)],
        pair(size + 6, depth) + conv_scratch(4) + pair(4 * breadth, 2 * depth, BF16)
        + pair(4 * breadth, depth),
        flags, hidden, h_left, h_ahead, *second_weights[:2], biases, scaled, *second_weights[4:6],
        name="second",
    )
    out_send, _ = lax.optimization_barrier((out_send, cot_got[1]))
    out_got = place.across(out_send)

    rim_shapes = [(size + 2 + breadth, depth), (size + 2, depth)]
    upper, grad_second, to_next, to_prev = call(
        functools.partial(back_second_kernel, tile=4),
        [(size + 4, breadth, depth), (size + 4, breadth, depth)] + rim_shapes,
        conv_scratch(4) + edges(breadth),
        flags, cot_mine, cot_got, slope_second, *second_weights[2:4],
        name="back_second",
    )
    groups = place.groups()

    def weight_scratch(kinds, taps):
        turned = [pltpu.VMEM((kinds, depth, 4 * breadth), BF16) for _ in range(2)]
        return buffers(4) + turned + [pltpu.VMEM((taps, depth, depth), F32)]

    def second_weights_grad(to_next, to_prev, grad_second):
        behind, after = place.to_next(to_next), place.to_prev(to_prev)
        grads = call(
            functools.partial(weight_kernel, tile=4, first=False),
            [(9, own, depth)] * 2 + [(1, depth)],
            weight_scratch(2, 9) + pair(size + 6, depth),
            flags, hidden, h_left, h_ahead, grad_second,
            name="weight_second", paired=True,
        )
        return behind, after, *grads

    behind, after, keep, send, gb_second = block(
        second_weights_grad, to_next, to_prev, grad_second
    )
    out_got, send = lax.optimization_barrier((out_got, send))

    def first_weights_grad(keep, send, upper, behind, after):
        grads = call(
            functools.partial(weight_kernel, tile=4, first=True),
            [(10, own, depth)] * 2 + [(1, depth)] * 2 + [(size + 2, breadth, depth)],
            weight_scratch(4, 10),
            flags, scaled, x_left, x_right, upper, behind, after, slope_first, cot_mine, cot_got,
            name="weight_first", paired=True,
        )
        return place.flip(send, groups[0][0]), *grads

    gw_second = [keep]
    other, keep, send, gb_first, gb_skip, grad_first = block(
        first_weights_grad, keep, send, upper, behind, after
    )
    gw_second = [value.reshape(-1, depth) for value in (*gw_second, other)]

    def input_grad(part, *before):
        shapes = [(size // 2, breadth, own)] * 2
        shapes += rim_shapes if part else [(32, depth)] * 2 + [(breadth, depth)]
        scratch = conv_scratch(13) + pair(13 * breadth, 2 * depth, BF16) + edges(40)
        return call(
            functools.partial(back_first_kernel, tile=13, part=part),
            shapes, scratch + [pltpu.VMEM((26, breadth, depth), F32)],
            flags, grad_first, cot_mine, cot_got, *first_weights[2:4], *second_weights[6:8], *before,
            name="back_first_%d" % part,
        )

    def upper_half(send, grad_first, *gw_second):
        return place.shared(gw_second, groups[1]), place.flip(send, groups[0][0]), *input_grad(0)

    gw_second, other, own_upper, send_upper, *before = block(upper_half, send, grad_first, *gw_second)
    gw_first = [value.reshape(-1, depth) for value in (keep, other)]
    got_upper = place.across(send_upper)

    def lower_half(gw_second, keep, other, *before):
        for bits in groups[2:]:
            gw_second = place.shared((gw_second,), bits)
        return gw_second, place.shared((keep, other), groups[1]), *input_grad(1, *before)

    gw_second, gw_first, own_lower, send_lower, to_next, to_prev = block(
        lower_half, gw_second, *gw_first, *before
    )
    got_lower = place.across(send_lower)
    lower_own, lower_send, lower_got = (own_upper, own_lower), (send_upper, send_lower), (got_upper, got_lower)

    def after_products(gw_first, gw_second, to_next, to_prev, out_own, out_got):
        behind, after = place.to_next(to_next), place.to_prev(to_prev)
        for bits in groups[2:]:
            gw_first = place.shared((gw_first,), bits)
        gw_second = gw_second[:, :own] + place.across(gw_second[:, own:])
        output, = call_copy(join_kernel, (rows, breadth, own), flags, out_own, out_got)
        return behind, after, gw_first, gw_second, output

    gw_first, gw_second, got_upper = lax.optimization_barrier((gw_first, gw_second, got_upper))
    behind, after, gw_first, gw_second, output = block(
        after_products, gw_first, gw_second, to_next, to_prev, out_own, out_got
    )

    def last_sums(gw_second, gw_first, behind, after, lower_own, lower_send):
        adds = jnp.concatenate([behind, after], axis=0)
        adds_got = place.across(adds[:, own:])
        column = jnp.arange(breadth)[None, :, None]
        row = jnp.arange(size)[:, None, None]
        edge = jnp.where(place.strip == 0, 0, size - 1)
        at_pole = place.side == 0

        def with_rims(value, adds):
            last = size + 2 + breadth
            value = value + jnp.where(column == 0, adds[1 : size + 1, None], 0.0)
            value = value + jnp.where(column == breadth - 1, adds[last + 1 : last + 1 + size, None], 0.0)
            return value + jnp.where((row == edge) & at_pole, adds[None, size + 2 : last], 0.0)

        sea_weight = sea_mask.astype(F32)[:, :, None]
        own_weight = lax.dynamic_slice_in_dim(sea_weight, place.half * size, size, 0)
        source = scaled[4 : size + 4]
        parts = []
        for value, lanes in ((lower_own, slice(0, own)), (lower_send, slice(own, depth))):
            value = with_rims(jnp.concatenate(value, axis=0), adds[:, lanes])
            parts.append(
                jnp.stack(
                    [
                        jnp.sum(own_weight * value, axis=(0, 1)),
                        jnp.sum(source[:, :, lanes] * value, axis=(0, 1)),
                    ]
                )
            )
        zeros = jnp.zeros((3, depth), F32)
        sums = [gb_first, gb_second, gb_skip, jnp.concatenate(parts, axis=1), zeros]
        sums = place.summed(jnp.concatenate(sums, axis=0))

        def collected(grad):
            for bits in reversed(groups[1:]):
                grad = place.spread(grad, bits)
            grad = grad.reshape(-1, own, own)
            return grad, place.flip(grad, groups[0][0])

        gw_first, _ = lax.optimization_barrier((gw_first, got_lower))
        gw_first = gw_first[:, :own] + place.across(gw_first[:, own:])
        gw_second, gw_first, gw_skip = gather_call(flags, *collected(gw_second), *collected(gw_first))
        sums = sums[:, :own] + place.across(sums[:, own:])
        adds_own = adds[:, :own]
        grad_half = final_call(0, flags, marked, lower_own, adds_own, stats, sums)
        return gw_second, gw_skip, gw_first, sums, adds_got, grad_half

    gw_second, gw_skip, gw_first, sums, adds_got, grad_half = last_sums(
        gw_second, gw_first, behind, after, lower_own, lower_send
    )
    late = (sums, gw_first, gw_second, gw_skip, grad_half, lower_got, adds_got)
    sums, gw_first, gw_second, gw_skip, grad_half, lower_got, adds_got = lax.optimization_barrier(late)
    grad_features = final_call(1, flags, marked, lower_got, adds_got, stats, sums, grad_half)
    new_mean = (1.0 - MOMENTUM) * run_mean + MOMENTUM * batch_mean
    new_var = (1.0 - MOMENTUM) * run_var + MOMENTUM * batch_var * sea_count / (sea_count - 1.0)
    return (
        output,
        grad_features,
        gw_first.reshape(3, 3, depth, own),
        sums[0],
        gw_second.reshape(3, 3, depth, own),
        sums[1],
        gw_skip,
        sums[2],
        new_mean,
        new_var,
    )


def solution(mesh):
    field, kernel, vector = P("pix", None, "ch"), P(None, None, None, "ch"), P("ch")
    placed = (
        field, P("pix", None), P(), kernel, vector, kernel, vector, P(None, "ch"), vector,
        vector, vector, field,
    )
    return jax.shard_map(
        functools.partial(local, mesh),
        mesh=mesh,
        in_specs=placed,
        out_specs=(
            field, field, kernel, vector, kernel, vector, P(None, "ch"), vector, vector, vector,
        ),
        check_vma=False,
    )
```

profile of v0, /device:TPU:0, one launch (start us, length us, event | category | flops | bytes accessed | tf_op | source)
XLA Modules:
  0.0 322.8 jit_solution(13018183177344106556)
XLA Ops:
  8.9 7.4 %pre.1 = (f32[96,64,128]{2,1,0:T(8,128)S(1)}, f32[52,64,128]{2,1,0:T(8,128)}, f32[8,128]{1,0:T(8,128)S(1)}, f32[4,64,128]{2,1,0:T(8,128)}, f32[160,128]{1,0:T(8,128)}, /*index=5*/f32[96,128]{1,0:T(8,128)}) custom-call(s32[6]{0:T(128)S(1)} %stack.84.flags, f32[96,64,128]{2,1,0:T(8,128)} %refs_0_, s32[64,96]{1,0:T(8,128)} %bitcast.58), custom_call_target="tpu_custom_call" | custom-call | tf_op jit(solution)/shard_map/pre/pallas_call | solution.py:911
  18.9 47.1 %conditional.7 = (f32[8,128]{1,0:T(8,128)}, f32[440,128]{1,0:T(8,128)}, f32[440,128]{1,0:T(8,128)}, f32[52,64,128]{2,1,0:T(8,128)}, f32[44,64,128]{2,1,0:T(8,128...) conditional(s32[]{:T(128)} %bitcast.5, () %tuple.86, ...), branch_computations={%region_1.2_spmd, %region_2.3_spmd} | conditional | flops 862217 | bytes 18006806 | solution.py:1134
  33.5 5.7 %cot.1 = (f32[52,64,128]{2,1,0:T(8,128)}, f32[44,64,128]{2,1,0:T(8,128)}, f32[8,64,128]{2,1,0:T(8,128)}) custom-call(s32[6]{0:T(128)S(1)} %get-tuple-element.156.flags, f32[96,64,128]{2,1,0:T(8,128)} %get-tuple-element.167.refs_0_, f32[2,64,128]{2,1,0:T(8,128)S(1)} %get-tuple-element.168.refs_1_), custom_call_target="tpu_custom_call" | custom-call | tf_op jit(solution)/shard_map/cond/branch_1_fun/cot/pallas_call | solution.py:911
  47.1 8.9 %collective-permute-done.23.refs_3_ = f32[1216,128]{1,0:T(8,128)} collective-permute-done((f32[1216,128]{1,0:T(8,128)}, f32[1216,128]{1,0:T(8,128)}, u32[]{:S(2)}, u32[]{:S(2)}) %collective-permute-start.23) | collective-permute-done | bytes 622624 | tf_op jit(solution)/shard_map/cond/branch_1_fun/ppermute | solution.py:954
  60.5 5.5 %weights_first.1 = (bf16[3,768,256]{2,1,0:T(8,128)(2,1)}, bf16[3,768,256]{2,1,0:T(8,128)(2,1)}, bf16[3,768,256]{2,1,0:T(8,128)(2,1)}, bf16[3,768,256]{2,1,0:T(8,128)(2,1)}) custom-call(s32[6]{0:T(128)S(1)} %get-tuple-element.156.flags, f32[2304,128]{1,0:T(8,128)} %get-tuple-element.175.refs_0_, f32[608,128]{1,0:T(8,128)} %slice.187.refs_1_, ...), custom_call_target="tpu_custom_call" | custom-call | tf_op jit(solution)/shard_map/cond/branch_1_fun/weights_first/pallas_call | solution.py:911
  68.8 20.1 %conditional.8 = ((f32[56,64,256]{2,1,0:T(8,128)}, f32[56,256]{1,0:T(8,128)}, f32[56,256]{1,0:T(8,128)}, f32[54,64,256]{2,1,0:T(8,128)}, f32[54,64,256]{2,1,0:T(...) conditional(s32[]{:T(128)} %bitcast.5, () %tuple.90, (s32[6]{0:T(128)S(1)}, f32[96,64,128]{2,1,0:T(8,128)S(1)}, ...), branch_computations={%region_3.4_spmd, %region_4.5_spmd} | conditional | bytes 11038812 | solution.py:1134
  68.8 20.1 %first.1 = (f32[56,64,256]{2,1,0:T(8,128)}, f32[56,256]{1,0:T(8,128)}, f32[56,256]{1,0:T(8,128)}, f32[54,64,256]{2,1,0:T(8,128)}, f32[54,64,256]{2,1,0:T(8,128)}, /*index=5*/f32[118,256]{1,0:T(8,128)}, f32[54,256]{1,0:T(8,128)}) custom-call(s32[6]{0:T(128)S(1)} %get-tuple-element.180.flags, f32[96,64,128]{2,1,0:T(8,128)S(1)} %get-tuple-element.181.refs_0_, ...), custom_call_target="tpu_custom_call" | custom-call | tf_op jit(solution)/shard_map/cond/branch_1_fun/first/pallas_call | solution.py:911
  91.7 6.5 %weights_second.1 = (bf16[3,768,256]{2,1,0:T(8,128)(2,1)}, bf16[3,768,256]{2,1,0:T(8,128)(2,1)}, bf16[3,768,256]{2,1,0:T(8,128)(2,1)}, bf16[3,768,256]{2,1,0:T(8...) custom-call(s32[6]{0:T(128)S(1)} %stack.84.flags, ...), custom_call_target="tpu_custom_call" | custom-call | tf_op jit(solution)/shard_map/weights_second/pallas_call | solution.py:911
  100.8 21.6 %second.1 = (f32[52,64,128]{2,1,0:T(8,128)}, f32[52,64,128]{2,1,0:T(8,128)}, f32[52,64,256]{2,1,0:T(8,128)}) custom-call(s32[6]{0:T(128)S(1)} %stack.84.flags, f32[54,64,256]{2,1,0:T(8,128)} %get-tuple-element.388.refs_0_, f32[54,256]{1,0:T(8,128)} %collective-permute-done.29.refs_1_, f32[118,256]{1,0:T(8,128)} %collective-permute-done.32.refs_2_, ...), custom_call_target="tpu_custom_call" | custom-call | tf_op jit(solution)/shard_map/second/pallas_call | solution.py:911
  123.9 20.7 %back_second.1 = (f32[52,64,256]{2,1,0:T(8,128)}, f32[52,64,256]{2,1,0:T(8,128)}, f32[114,256]{1,0:T(8,128)S(1)}, f32[50,256]{1,0:T(8,128)S(1)}) custom-call(s32[6]{0:T(128)S(1)} %stack.84.flags, f32[52,64,128]{2,1,0:T(8,128)} %get-tuple-element.375.refs_0_, f32[44,64,128]{2,1,0:T(8,128)} %collective-permute-done.30.refs_1_, ...), custom_call_target="tpu_custom_call" | custom-call | tf_op jit(solution)/shard_map/back_second/pallas_call | solution.py:911
  144.6 21.9 %conditional.9 = (f32[114,256]{1,0:T(8,128)}, f32[50,256]{1,0:T(8,128)}, f32[9,128,256]{2,1,0:T(8,128)}, f32[1,256]{1,0:T(1,128)S(1)}, f32[1152,256]{1,0:T(8,128)S(1)}) conditional(s32[]{:T(128)} %bitcast.5, () %tuple.85, (f32[114,256]{1,0:T(8,128)S(1)}, f32[50,256]{1,0:T(8,128)S(1)}, s32[6]{0:T(128)S(1)}, f32[54,64,256]{2,1,0:T(8,128)}, ...), branch_computations={%region_5.6_spmd, %region_6.7_spmd} | conditional | bytes 2528316 | solution.py:1134
  147.6 18.8 %weight_second.1 = (f32[9,128,256]{2,1,0:T(8,128)S(1)}, f32[9,128,256]{2,1,0:T(8,128)}, f32[1,256]{1,0:T(1,128)S(1)}) custom-call(s32[6]{0:T(128)S(1)} %get-tuple-element.190.flags, f32[54,64,256]{2,1,0:T(8,128)} %get-tuple-element.191.refs_0_, f32[54,256]{1,0:T(8,128)} %get-tuple-element.192.refs_1_, f32[118,256]{1,0:T(8,128)} %get-tuple-element.193.refs_2_, ...), custom_call_target="tpu_custom_call" | custom-call | tf_op jit(solution)/shard_map/cond/branch_1_fun/weight_second/pallas_call | solution.py:911
  166.5 24.0 %conditional.10 = (f32[10,128,256]{2,1,0:T(8,128)}, f32[1,256]{1,0:T(1,128)S(1)}, f32[1,256]{1,0:T(1,128)S(1)}, f32[50,64,256]{2,1,0:T(8,128)}, f32[1152,256]{1,0:T(8,128)}, /*index=5*/f32[1280,256]{1,0:T(8,128)}) conditional(s32[]{:T(128)} %bitcast.5, () %tuple.95, (s32[6]{0:T(128)S(1)}, f32[56,64,256]{2,1,0:T(8,128)}, f32[56,256]{1,0:T(8,128)S(1)}, ...), branch_computations={%region_7.8_spmd, %region_8.9_spmd} | conditional | bytes 7080008 | solution.py:1134
  166.7 23.9 %weight_first.1 = (f32[10,128,256]{2,1,0:T(8,128)}, f32[10,128,256]{2,1,0:T(8,128)}, f32[1,256]{1,0:T(1,128)S(1)}, f32[1,256]{1,0:T(1,128)S(1)}, f32[50,64,256]{2,1,0:T(8,128)}) custom-call(s32[6]{0:T(128)S(1)} %get-tuple-element.198.flags, f32[56,64,256]{2,1,0:T(8,128)} %get-tuple-element.199.refs_0_, f32[56,256]{1,0:T(8,128)S(1)} %get-tuple-element.200.refs_1_, ...), custom_call_target="tpu_custom_call" | custom-call | tf_op jit(solution)/shard_map/cond/branch_1_fun/weight_first/pallas_call | solution.py:911
  190.6 20.3 %conditional.11 = (f32[576,256]{1,0:T(8,128)S(1)}, f32[24,64,128]{2,1,0:T(8,128)S(1)}, f32[24,64,128]{2,1,0:T(8,128)}, f32[32,256]{1,0:T(8,128)S(1)}, f32[32,256...) conditional(s32[]{:T(128)} %bitcast.5, () %tuple.84, (s32[]{:T(128)}, f32[1152,256]{1,0:T(8,128)S(1)}, ...), branch_computations={%region_9.10_spmd, %region_10.11_spmd} | conditional | flops 442381 | bytes 17498454 | solution.py:1134
  194.1 15.2 %back_first_0.1 = (f32[24,64,128]{2,1,0:T(8,128)S(1)}, f32[24,64,128]{2,1,0:T(8,128)}, f32[32,256]{1,0:T(8,128)S(1)}, f32[32,256]{1,0:T(8,128)}, f32[64,256]{1,0:T(8,128)}) custom-call(s32[6]{0:T(128)S(1)} %get-tuple-element.218.flags, f32[50,64,256]{2,1,0:T(8,128)} %get-tuple-element.219.refs_0_, f32[52,64,128]{2,1,0:T(8,128)S(1)} %get-tuple-element.220.refs_1_, ...), custom_call_target="tpu_custom_call" | custom-call | tf_op jit(solution)/shard_map/cond/branch_1_fun/back_first_0/pallas_call | solution.py:911
  214.2 27.8 %conditional.12 = (f32[144,256]{1,0:T(8,128)S(1)}, f32[640,256]{1,0:T(8,128)}, f32[24,64,128]{2,1,0:T(8,128)S(1)}, f32[24,64,128]{2,1,0:T(8,128)}, f32[114,256]{1,0:T(8,128)}, /*index=5*/f32[50,256]{1,0:T(8,128)}) conditional(s32[]{:T(128)} %bitcast.5, () %tuple.83, (s32[]{:T(128)}, f32[576,256]{1,0:T(8,128)S(1)}, f32[1280,256]{1,0:T(8,128)}, ...), branch_computations={%region_11.12_spmd, %region_12.13_spmd} | conditional | flops 602153 | bytes 13222626 | solution.py:1134
  223.1 15.3 %back_first_1.1 = (f32[24,64,128]{2,1,0:T(8,128)S(1)}, f32[24,64,128]{2,1,0:T(8,128)}, f32[114,256]{1,0:T(8,128)}, f32[50,256]{1,0:T(8,128)}) custom-call(s32[6]{0:T(128)S(1)} %get-tuple-element.237.flags, f32[50,64,256]{2,1,0:T(8,128)} %get-tuple-element.238.refs_0_, f32[52,64,128]{2,1,0:T(8,128)S(1)} %get-tuple-element.239.refs_1_, ...), custom_call_target="tpu_custom_call" | custom-call | tf_op jit(solution)/shard_map/cond/branch_1_fun/back_first_1/pallas_call | solution.py:911
  242.0 21.2 %conditional.13 = (f32[114,256]{1,0:T(8,128)}, f32[50,256]{1,0:T(8,128)}, f32[160,256]{1,0:T(8,128)S(1)}, f32[144,128]{1,0:T(8,128)S(1)}, f32[96,64,128]{2,1,0:T(8,128)}) conditional(s32[]{:T(128)} %bitcast.5, () %tuple.82, (f32[114,256]{1,0:T(8,128)}, f32[50,256]{1,0:T(8,128)}, s32[]{:T(128)}, f32[640,256]{1,0:T(8,128)}, ...), branch_computations={%region_13.14_spmd, %region_14.15_spmd} | conditional | flops 141340 | bytes 5104220 | solution.py:1134
  255.7 6.5 %collective-permute-done.12 = f32[160,256]{1,0:T(8,128)S(1)} collective-permute-done((f32[160,256]{1,0:T(8,128)S(1)}, f32[160,256]{1,0:T(8,128)S(1)}, u32[]{:S(2)}, u32[]{:S(2)}) %collective-permute-start.12) | collective-permute-done | bytes 163872 | tf_op jit(solution)/shard_map/cond/branch_1_fun/ppermute | solution.py:990
  266.3 3.7 %multiply_reduce_fusion.2 = (f32[128]{0:T(128)S(1)}, f32[128]{0:T(128)S(1)}, f32[128]{0:T(128)S(1)}, f32[128]{0:T(128)S(1)}) fusion(f32[56,64,256]{2,1,0:T(8,128)} %get-tuple-element.397.refs_6_, f32[64,128]{1,0:T(8,128)S(1)} %get-tuple-element.508, pred[48]{0:T(512)(128)(4,1)S(1)} %copy-done.25, f32[48,128]{1,0:T(8,128)S(1)} %get-tuple-element.510, ...), kind=kLoop, calls=%fused_computation.46 | loop fusion | flops 8650240 | bytes 6469808 | tf_op jit(solution)/shard_map/reduce_sum | solution.py:1306
  298.7 5.2 %collective-permute-done.50 = f32[640,128]{1,0:T(8,128)S(1)} collective-permute-done((f32[640,128]{1,0:T(8,128)S(1)}, f32[640,128]{1,0:T(8,128)S(1)}, u32[]{:S(2)}, u32[]{:S(2)}) %collective-permute-start.50) | collective-permute-done | bytes 327712 | tf_op jit(solution)/shard_map/ppermute | solution.py:996
  310.5 3.7 %final_own.1.rest_0_ = f32[96,64,128]{2,1,0:T(8,128)} custom-call(s32[6]{0:T(128)S(1)} %stack.84.flags, f32[96,64,128]{2,1,0:T(8,128)S(1)} %copy-done.3, f32[24,64,128]{2,1,0:T(8,128)S(1)} %get-tuple-element.443.lower_upper, f32[24,64,128]{2,1,0:T(8,128)} %copy-done.4, f32[164,128]{1,0:T(8,128)} %get-tuple-element.504.rims, ...), custom_call_target="tpu_custom_call" | custom-call | bytes 9437184 | tf_op jit(solution)/shard_map/final_own/pallas_call | solution.py:787
  318.7 3.9 %final_got.1 = f32[96,64,128]{2,1,0:T(8,128)} custom-call(s32[6]{0:T(128)S(1)} %stack.84.flags, f32[96,64,128]{2,1,0:T(8,128)S(1)} %copy-done.3, f32[24,64,128]{2,1,0:T(8,128)} %collective-permute-done.34.lower_upper, f32[24,64,128]{2,1,0:T(8,128)} %copy-done.9, f32[164,128]{1,0:T(8,128)} %copy-done.17, ...), custom_call_target="tpu_custom_call", output_to_operand_aliasing={{}: (7, {})} | custom-call | bytes 9437184 | tf_op jit(solution)/shard_map/final_got/pallas_call | solution.py:787
  (236 shorter events, 126.2 us)
Async XLA Ops:
  3.1 13.3 %collective-permute-start.26 = (f32[616,128]{1,0:T(8,128)S(1)}, f32[616,128]{1,0:T(8,128)}, u32[]{:S(2)}, u32[]{:S(2)}) collective-permute-start(f32[616,128]{1,0:T(8,128)S(1)} %pad_maximum_fusion.6), channel_id=1, source_target_pairs={{0,1},{1,0},{2,3},{3,2},{4,5},{5,4},{6,7},{7,6},{8,9},{9,8},{10,11... | collective-permute-start | bytes 946184 | tf_op jit(solution)/shard_map/ppermute | solution.py:951
  16.4 49.6 %collective-permute-start.28 = (f32[52,64,128]{2,1,0:T(8,128)}, f32[52,64,128]{2,1,0:T(8,128)}, u32[]{:S(2)}, u32[]{:S(2)}) collective-permute-start(f32[52,64,128]{2,1,0:T(8,128)} %get-tuple-element.378), channel_id=1, source_target_pairs={{0,1},{1,0},{2,3},{3,2},{4,5},{5,4},{6,7},{7,6},{8,9},{9,8},{10,11... | collective-permute-start | bytes 5111816 | tf_op jit(solution)/shard_map/ppermute | solution.py:951
  27.9 11.4 %collective-permute-start.19 = (f32[608,128]{1,0:T(8,128)}, f32[608,128]{1,0:T(8,128)}, u32[]{:S(2)}, u32[]{:S(2)}) collective-permute-start(f32[608,128]{1,0:T(8,128)} %slice.187.refs_1_), channel_id=1, source_target_pairs={{0,8},{2,10},{4,12},{6,14},{8,0},{10,2},{12,4},{14,6},{16,24},{18,... | collective-permute-start | bytes 933896 | tf_op jit(solution)/shard_map/cond/branch_1_fun/ppermute | solution.py:954
  41.3 14.7 %collective-permute-start.23 = (f32[1216,128]{1,0:T(8,128)}, f32[1216,128]{1,0:T(8,128)}, u32[]{:S(2)}, u32[]{:S(2)}) collective-permute-start(f32[1216,128]{1,0:T(8,128)} %pad_maximum_fusion.1), channel_id=1, source_target_pairs={{0,4},{2,6},{4,0},{6,2},{8,12},{10,14},{12,8},{14,10},{16,20},{18,... | collective-permute-start | bytes 1867784 | tf_op jit(solution)/shard_map/cond/branch_1_fun/ppermute | solution.py:954
  66.0 34.8 %collective-permute-start.30 = (f32[44,64,128]{2,1,0:T(8,128)}, f32[44,64,128]{2,1,0:T(8,128)}, u32[]{:S(2)}, u32[]{:S(2)}) collective-permute-start(f32[44,64,128]{2,1,0:T(8,128)} %get-tuple-element.385), channel_id=1, source_target_pairs={{0,1},{1,0},{2,3},{3,2},{4,5},{5,4},{6,7},{7,6},{8,9},{9,8},{10,11... | collective-permute-start | bytes 4325384 | tf_op jit(solution)/shard_map/ppermute | solution.py:951
  67.4 55.0 %collective-permute-start.31 = (f32[8,64,128]{2,1,0:T(8,128)}, f32[8,64,128]{2,1,0:T(8,128)S(1)}, u32[]{:S(2)}, u32[]{:S(2)}) collective-permute-start(f32[8,64,128]{2,1,0:T(8,128)} %get-tuple-element.387), channel_id=1, source_target_pairs={{0,1},{1,0},{2,3},{3,2},{4,5},{5,4},{6,7},{7,6},{8,9},{9,8},{10,11... | collective-permute-start | bytes 786440 | tf_op jit(solution)/shard_map/ppermute | solution.py:951
  88.9 11.9 %collective-permute-start.32 = (f32[118,256]{1,0:T(8,128)}, f32[118,256]{1,0:T(8,128)}, u32[]{:S(2)}, u32[]{:S(2)}) collective-permute-start(f32[118,256]{1,0:T(8,128)} %get-tuple-element.390), channel_id=1, source_target_pairs={{0,12},{2,14},{4,0},{6,2},{8,4},{10,6},{12,8},{14,10},{16,28},{18,... | collective-permute-start | bytes 362504 | tf_op jit(solution)/shard_map/ppermute | solution.py:948
  122.5 44.0 %collective-permute-start.33 = (f32[52,64,128]{2,1,0:T(8,128)}, f32[52,64,128]{2,1,0:T(8,128)}, u32[]{:S(2)}, u32[]{:S(2)}) collective-permute-start(f32[52,64,128]{2,1,0:T(8,128)} %get-tuple-element.414), channel_id=1, source_target_pairs={{0,1},{1,0},{2,3},{3,2},{4,5},{5,4},{6,7},{7,6},{8,9},{9,8},{10,11... | collective-permute-start | bytes 5111816 | tf_op jit(solution)/shard_map/ppermute | solution.py:951
  144.7 21.8 %collective-permute-start = (f32[114,256]{1,0:T(8,128)S(1)}, f32[114,256]{1,0:T(8,128)}, u32[]{:S(2)}, u32[]{:S(2)}) collective-permute-start(f32[114,256]{1,0:T(8,128)S(1)} %get-tuple-element.188), channel_id=1, source_target_pairs={{0,4},{2,6},{4,8},{6,10},{8,12},{10,14},{12,0},{14,2},{16,20},{18,... | collective-permute-start | bytes 350216 | tf_op jit(solution)/shard_map/cond/branch_1_fun/ppermute | solution.py:945
  146.4 20.1 %collective-permute-start.1 = (f32[50,256]{1,0:T(8,128)S(1)}, f32[50,256]{1,0:T(8,128)}, u32[]{:S(2)}, u32[]{:S(2)}) collective-permute-start(f32[50,256]{1,0:T(8,128)S(1)} %get-tuple-element.189), channel_id=1, source_target_pairs={{0,12},{2,14},{4,0},{6,2},{8,4},{10,6},{12,8},{14,10},{16,28},{18,... | collective-permute-start | bytes 153608 | tf_op jit(solution)/shard_map/cond/branch_1_fun/ppermute | solution.py:948
  166.6 24.0 %collective-permute-start.2 = (f32[9,128,256]{2,1,0:T(8,128)}, f32[9,128,256]{2,1,0:T(8,128)}, u32[]{:S(2)}, u32[]{:S(2)}) collective-permute-start(f32[9,128,256]{2,1,0:T(8,128)} %get-tuple-element.213), channel_id=1, source_target_pairs={{0,2},{2,0},{4,6},{6,4},{8,10},{10,8},{12,14},{14,12},{16,18},{18,... | collective-permute-start | bytes 3538952 | tf_op jit(solution)/shard_map/cond/branch_1_fun/ppermute | solution.py:954
  190.8 20.1 %collective-permute-start.4 = (f32[10,128,256]{2,1,0:T(8,128)}, f32[10,128,256]{2,1,0:T(8,128)}, u32[]{:S(2)}, u32[]{:S(2)}) collective-permute-start(f32[10,128,256]{2,1,0:T(8,128)} %get-tuple-element.232), channel_id=1, source_target_pairs={{0,2},{2,0},{4,6},{6,4},{8,10},{10,8},{12,14},{14,12},{16,18},{18,... | collective-permute-start | bytes 3932168 | tf_op jit(solution)/shard_map/cond/branch_1_fun/ppermute | solution.py:954
  193.4 16.0 %collective-permute-start.3 = (f32[576,256]{1,0:T(8,128)}, f32[576,256]{1,0:T(8,128)}, u32[]{:S(2)}, u32[]{:S(2)}) collective-permute-start(f32[576,256]{1,0:T(8,128)} %dynamic-slice_add_fusion), channel_id=1, source_target_pairs={{0,4},{2,6},{4,0},{6,2},{8,12},{10,14},{12,8},{14,10},{16,20},{18,... | collective-permute-start | bytes 1769480 | tf_op jit(solution)/shard_map/cond/branch_1_fun/ppermute | solution.py:990
  210.9 31.1 %collective-permute-start.34 = (f32[24,64,128]{2,1,0:T(8,128)}, f32[24,64,128]{2,1,0:T(8,128)}, u32[]{:S(2)}, u32[]{:S(2)}) collective-permute-start(f32[24,64,128]{2,1,0:T(8,128)} %get-tuple-element.434), channel_id=1, source_target_pairs={{0,1},{1,0},{2,3},{3,2},{4,5},{5,4},{6,7},{7,6},{8,9},{9,8},{10,11... | collective-permute-start | bytes 2359304 | tf_op jit(solution)/shard_map/ppermute | solution.py:951
  216.6 22.9 %collective-permute-start.8 = (f32[640,256]{1,0:T(8,128)}, f32[640,256]{1,0:T(8,128)}, u32[]{:S(2)}, u32[]{:S(2)}) collective-permute-start(f32[640,256]{1,0:T(8,128)} %dynamic-slice_add_fusion.1), channel_id=1, source_target_pairs={{0,4},{2,6},{4,0},{6,2},{8,12},{10,14},{12,8},{14,10},{16,20},{18,... | collective-permute-start | bytes 1966088 | tf_op jit(solution)/shard_map/cond/branch_1_fun/ppermute | solution.py:990
  218.7 19.7 %collective-permute-start.7 = (f32[144,256]{1,0:T(8,128)}, f32[144,256]{1,0:T(8,128)}, u32[]{:S(2)}, u32[]{:S(2)}) collective-permute-start(f32[144,256]{1,0:T(8,128)} %get-tuple-element.475), channel_id=1, source_target_pairs={{0,24},{2,26},{4,28},{6,30},{8,16},{10,18},{12,20},{14,22},{16,8},... | collective-permute-start | bytes 442376 | tf_op jit(solution)/shard_map/cond/branch_1_fun/ppermute | solution.py:990
  220.2 18.1 %collective-permute-start.6 = (f32[144,256]{1,0:T(8,128)}, f32[144,256]{1,0:T(8,128)}, u32[]{:S(2)}, u32[]{:S(2)}) collective-permute-start(f32[144,256]{1,0:T(8,128)} %get-tuple-element.476), channel_id=1, source_target_pairs={{0,16},{2,18},{4,20},{6,22},{8,24},{10,26},{12,28},{14,30},{16,0},... | collective-permute-start | bytes 442376 | tf_op jit(solution)/shard_map/cond/branch_1_fun/ppermute | solution.py:990
  221.6 16.7 %collective-permute-start.5 = (f32[144,256]{1,0:T(8,128)}, f32[144,256]{1,0:T(8,128)}, u32[]{:S(2)}, u32[]{:S(2)}) collective-permute-start(f32[144,256]{1,0:T(8,128)} %get-tuple-element.474), channel_id=1, source_target_pairs={{0,8},{2,10},{4,12},{6,14},{8,0},{10,2},{12,4},{14,6},{16,24},{18,... | collective-permute-start | bytes 442376 | tf_op jit(solution)/shard_map/cond/branch_1_fun/ppermute | solution.py:990
  242.1 21.2 %collective-permute-start.9 = (f32[114,256]{1,0:T(8,128)}, f32[114,256]{1,0:T(8,128)}, u32[]{:S(2)}, u32[]{:S(2)}) collective-permute-start(f32[114,256]{1,0:T(8,128)} %get-tuple-element.253), channel_id=1, source_target_pairs={{0,4},{2,6},{4,8},{6,10},{8,12},{10,14},{12,0},{14,2},{16,20},{18,... | collective-permute-start | bytes 350216 | tf_op jit(solution)/shard_map/cond/branch_1_fun/ppermute | solution.py:945
  242.9 20.3 %collective-permute-start.10 = (f32[50,256]{1,0:T(8,128)}, f32[50,256]{1,0:T(8,128)}, u32[]{:S(2)}, u32[]{:S(2)}) collective-permute-start(f32[50,256]{1,0:T(8,128)} %get-tuple-element.254), channel_id=1, source_target_pairs={{0,12},{2,14},{4,0},{6,2},{8,4},{10,6},{12,8},{14,10},{16,28},{18,... | collective-permute-start | bytes 153608 | tf_op jit(solution)/shard_map/cond/branch_1_fun/ppermute | solution.py:948
  249.1 13.1 %collective-permute-start.12 = (f32[160,256]{1,0:T(8,128)S(1)}, f32[160,256]{1,0:T(8,128)S(1)}, u32[]{:S(2)}, u32[]{:S(2)}) collective-permute-start(f32[160,256]{1,0:T(8,128)S(1)} %get-tuple-element.479), channel_id=1, source_target_pairs={{0,16},{2,18},{4,20},{6,22},{8,24},{10,26},{12,28},{14,30},{16,0},... | collective-permute-start | bytes 491528 | tf_op jit(solution)/shard_map/cond/branch_1_fun/ppermute | solution.py:990
  263.2 17.9 %collective-permute-start.45 = (f32[24,64,128]{2,1,0:T(8,128)}, f32[24,64,128]{2,1,0:T(8,128)S(1)}, u32[]{:S(2)}, u32[]{:S(2)}) collective-permute-start(f32[24,64,128]{2,1,0:T(8,128)} %get-tuple-element.447), channel_id=1, source_target_pairs={{0,1},{1,0},{2,3},{3,2},{4,5},{5,4},{6,7},{7,6},{8,9},{9,8},{10,11... | collective-permute-start | bytes 2359304 | tf_op jit(solution)/shard_map/ppermute | solution.py:951
  281.7 24.6 %collective-permute-start.38 = (f32[8,256]{1,0:T(8,128)S(1)}, f32[8,256]{1,0:T(8,128)S(1)}, u32[]{:S(2)}, u32[]{:S(2)}) collective-permute-start(f32[8,256]{1,0:T(8,128)S(1)} %select_add_fusion.1), channel_id=1, source_target_pairs={{0,16},{2,18},{4,20},{6,22},{8,24},{10,26},{12,28},{14,30},{16,0},... | collective-permute-start | bytes 24584 | tf_op jit(solution)/shard_map/ppermute | solution.py:954
  298.7 15.5 %collective-permute-start.44 = (f32[9,128,128]{2,1,0:T(8,128)}, f32[9,128,128]{2,1,0:T(8,128)}, u32[]{:S(2)}, u32[]{:S(2)}) collective-permute-start(f32[9,128,128]{2,1,0:T(8,128)} %bitcast.24.second_mine), channel_id=1, source_target_pairs={{0,2},{2,0},{4,6},{6,4},{8,10},{10,8},{12,14},{14,12},{16,18},{18,... | collective-permute-start | bytes 1769480 | tf_op jit(solution)/shard_map/ppermute | solution.py:954
  (58 other events, 749.3 us)
where the time goes:
time: 324 us; the launch traced here: 323 us
  Pallas kernels  177 us (55%)
  starting transfers between devices  57.2 us (18%)
  waiting for transfers between devices  44.2 us (14%)
  other arithmetic  27.5 us (8%)
  local copies, waits for them, and re-layouts  13 us (4%)
  between operations  3.28 us (1%)
    pallas_call x12, Pallas kernels, call(): pl.pallas_call(body, out_shape=shapes, in_specs=[pl.BlockSpec(memory_spac...  163 us
    ppermute x17, waiting for transfers between devices, flip(): return lax.ppermute(value, 'pix', [(i, i ^ bit) for i in range(self.count)])  18.3 us
    ppermute x8, waiting for transfers between devices, spread(): lax.ppermute(value, 'pix', pairs)  13.8 us
    ppermute x12, starting transfers between devices, across(): return lax.ppermute(value, 'ch', [(0, 1), (1, 0)])  13.5 us
    ppermute x17, starting transfers between devices, flip(): return lax.ppermute(value, 'pix', [(i, i ^ bit) for i in range(self.count)])  11.2 us
    ppermute x8, starting transfers between devices, shared(): parts.append(lax.ppermute(piece, 'pix', pairs))  10.9 us
    ppermute x8, starting transfers between devices, spread(): lax.ppermute(value, 'pix', pairs)  10.3 us
    ppermute x4, starting transfers between devices, to_prev(): return lax.ppermute(value, 'pix', self.ribbon_pairs(-1))  8.7 us
  transfers between devices with their start and end apart: 53, of which 18 were waited for; matrix products, arithmetic and copies ran while one was open for 11% of the time, Pallas kernels for 54%

commit v1 on v0

--- a/solution.py
+++ b/solution.py
@@ -1090,12 +1090,14 @@
     cot_inner = place.inner_rows(cotangent, 2)
 
     def neighbours(stats, inner, to_prev, to_next, message):
-        mine = message[: 2 * share + share_skip]
+        mine = message
         bits = place.near()
         ahead, behind = place.to_prev(to_prev), place.to_next(to_next)
         shares = [mine, place.flip(mine, bits[2])]
         shares[1], ahead, behind = lax.optimization_barrier((shares[1], ahead, behind))
-        shares.append(place.flip(jnp.concatenate(shares, axis=0), bits[1]))
+        both = jnp.concatenate(shares, axis=0)
+        both, inner_rows = lax.optimization_barrier((both, cot_inner))
+        shares.append(place.flip(both, bits[1]))
 
         def inner_part(value):
             return jnp.where(place.strip == 0, value[rows - 4 : rows], value[:4])
@@ -1112,7 +1114,7 @@
         late = size // 6
         cot_mine, cot_early, cot_late = call(
             cot_kernel, [(size + 4, breadth, own), (size + 4 - late, breadth, own), (late, breadth, own)],
-            [], flags, cotangent, cot_inner, name="cot",
+            [], flags, cotangent, inner_rows, name="cot",
         )
         gate = (shares[2], halo_theirs, cot_early)
         shares[2], halo_theirs, cot_early = lax.optimization_barrier(gate)
@@ -1314,23 +1316,22 @@
         def collected(grad):
             for bits in reversed(groups[1:]):
                 grad = place.spread(grad, bits)
-            grad = grad.reshape(-1, own, own)
-            return grad, place.flip(grad, groups[0][0])
+            return grad.reshape(-1, own, own)
 
         gw_first, _ = lax.optimization_barrier((gw_first, got_lower))
         gw_first = gw_first[:, :own] + place.across(gw_first[:, own:])
-        gw_second, gw_first, gw_skip = gather_call(flags, *collected(gw_second), *collected(gw_first))
+        gw_second, gw_first = collected(gw_second), collected(gw_first)
+        second_other = place.flip(gw_second, groups[0][0])
         sums = sums[:, :own] + place.across(sums[:, own:])
-        adds_own = adds[:, :own]
-        grad_half = final_call(0, flags, marked, lower_own, adds_own, stats, sums)
-        return gw_second, gw_skip, gw_first, sums, adds_got, grad_half
-
-    gw_second, gw_skip, gw_first, sums, adds_got, grad_half = last_sums(
+        grad_half = final_call(0, flags, marked, lower_own, adds[:, :own], stats, sums)
+
+        first_other = place.flip(gw_first, groups[0][0])
+        grad_features = final_call(1, flags, marked, lower_got, adds_got, stats, sums, grad_half)
+        return sums, grad_features, *gather_call(flags, gw_second, second_other, gw_first, first_other)
+
+    sums, grad_features, gw_second, gw_first, gw_skip = last_sums(
         gw_second, gw_first, behind, after, lower_own, lower_send
     )
-    late = (sums, gw_first, gw_second, gw_skip, grad_half, lower_got, adds_got)
-    sums, gw_first, gw_second, gw_skip, grad_half, lower_got, adds_got = lax.optimization_barrier(late)
-    grad_features = final_call(1, flags, marked, lower_got, adds_got, stats, sums, grad_half)
     new_mean = (1.0 - MOMENTUM) * run_mean + MOMENTUM * batch_mean
     new_var = (1.0 - MOMENTUM) * run_var + MOMENTUM * batch_var * sea_count / (sea_count - 1.0)
     return (

time: 324 us -> 321 us (level)
    ppermute x17, waiting for transfers between devices: 18.3 us -> 11.6 us  [flip(): return lax.ppermute(value, 'pix', [(i, i ^ bit) for i in range(self.count)])]
    ppermute x4, waiting for transfers between devices: 0.01 us -> 5.3 us  [to_next(): return lax.ppermute(value, 'pix', self.ribbon_pairs(1))]
  transfers between devices with their start and end apart: 53 -> 53, of which waited for: 18 -> 19; matrix products, arithmetic and copies ran while one was open for 11% -> 12% of each run, Pallas kernels for 54% -> 55%
where the time goes in v1:
time: 321 us; the launch traced here: 320 us
  Pallas kernels  178 us (55%)
  starting transfers between devices  55.1 us (17%)
  waiting for transfers between devices  42 us (13%)
  other arithmetic  30.1 us (9%)
  local copies, waits for them, and re-layouts  10.7 us (3%)
  between operations  3.3 us (1%)
    pallas_call x12, Pallas kernels, call(): pl.pallas_call(body, out_shape=shapes, in_specs=[pl.BlockSpec(memory_spac...  164 us
    ppermute x12, starting transfers between devices, across(): return lax.ppermute(value, 'ch', [(0, 1), (1, 0)])  13.6 us
    ppermute x8, waiting for transfers between devices, spread(): lax.ppermute(value, 'pix', pairs)  13.6 us
    ppermute x17, waiting for transfers between devices, flip(): return lax.ppermute(value, 'pix', [(i, i ^ bit) for i in range(self.count)])  11.6 us
    ppermute x8, starting transfers between devices, spread(): lax.ppermute(value, 'pix', pairs)  10.6 us
    ppermute x8, starting transfers between devices, shared(): parts.append(lax.ppermute(piece, 'pix', pairs))  10.3 us
    ppermute x17, starting transfers between devices, flip(): return lax.ppermute(value, 'pix', [(i, i ^ bit) for i in range(self.count)])  10.1 us
    ppermute x4, starting transfers between devices, to_prev(): return lax.ppermute(value, 'pix', self.ribbon_pairs(-1))  8.08 us
  transfers between devices with their start and end apart: 53, of which 19 were waited for; matrix products, arithmetic and copies ran while one was open for 12% of the time, Pallas kernels for 55%

profile of v1, /device:TPU:0, one launch (start us, length us, event | category | flops | bytes accessed | tf_op | source)
XLA Modules:
  0.0 320.0 jit_solution(14084541394090243324)
XLA Ops:
  9.6 7.4 %pre.1 = (f32[96,64,128]{2,1,0:T(8,128)S(1)}, f32[52,64,128]{2,1,0:T(8,128)}, f32[8,128]{1,0:T(8,128)S(1)}, f32[4,64,128]{2,1,0:T(8,128)}, f32[160,128]{1,0:T(8,128)}, /*index=5*/f32[96,128]{1,0:T(8,128)}) custom-call(s32[6]{0:T(128)S(1)} %stack.84.flags, f32[96,64,128]{2,1,0:T(8,128)} %refs_0_, s32[64,96]{1,0:T(8,128)} %bitcast.58), custom_call_target="tpu_custom_call" | custom-call | tf_op jit(solution)/shard_map/pre/pallas_call | solution.py:911
  19.5 45.7 %conditional.7 = (f32[8,128]{1,0:T(8,128)S(1)}, f32[440,128]{1,0:T(8,128)}, f32[440,128]{1,0:T(8,128)}, f32[52,64,128]{2,1,0:T(8,128)}, f32[44,64,128]{2,1,0:T(8...) conditional(s32[]{:T(128)} %bitcast.5, () %tuple.86, ...), branch_computations={%region_1.2_spmd, %region_2.3_spmd} | conditional | flops 872457 | bytes 17212182 | solution.py:1136
  34.1 5.3 %collective-permute-done.21.refs_0_ = f32[96,128]{1,0:T(8,128)} collective-permute-done((f32[96,128]{1,0:T(8,128)}, f32[96,128]{1,0:T(8,128)}, u32[]{:S(2)}, u32[]{:S(2)}) %collective-permute-start.21) | collective-permute-done | bytes 49184 | tf_op jit(solution)/shard_map/cond/branch_1_fun/ppermute | solution.py:945
  45.3 6.0 %cot.1 = (f32[52,64,128]{2,1,0:T(8,128)}, f32[44,64,128]{2,1,0:T(8,128)}, f32[8,64,128]{2,1,0:T(8,128)}) custom-call(s32[6]{0:T(128)S(1)} %get-tuple-element.156.flags, f32[96,64,128]{2,1,0:T(8,128)} %get-tuple-element.169.refs_0_, f32[2,64,128]{2,1,0:T(8,128)} %copy-done.21), custom_call_target="tpu_custom_call" | custom-call | tf_op jit(solution)/shard_map/cond/branch_1_fun/cot/pallas_call | solution.py:911
  59.7 5.5 %weights_first.1 = (bf16[3,768,256]{2,1,0:T(8,128)(2,1)}, bf16[3,768,256]{2,1,0:T(8,128)(2,1)}, bf16[3,768,256]{2,1,0:T(8,128)(2,1)}, bf16[3,768,256]{2,1,0:T(8,128)(2,1)}) custom-call(s32[6]{0:T(128)S(1)} %get-tuple-element.156.flags, f32[2304,128]{1,0:T(8,128)} %get-tuple-element.177.refs_0_, f32[616,128]{1,0:T(8,128)S(1)} %get-tuple-element.528.refs_1_, ...), custom_call_target="tpu_custom_call" | custom-call | tf_op jit(solution)/shard_map/cond/branch_1_fun/weights_first/pallas_call | solution.py:911
  68.0 20.1 %conditional.8 = ((f32[56,64,256]{2,1,0:T(8,128)}, f32[56,256]{1,0:T(8,128)S(1)}, f32[56,256]{1,0:T(8,128)S(1)}, f32[54,64,256]{2,1,0:T(8,128)}, f32[54,64,256]{...) conditional(s32[]{:T(128)} %bitcast.5, () %tuple.90, (s32[6]{0:T(128)S(1)}, f32[96,64,128]{2,1,0:T(8,128)S(1)}, ...), branch_computations={%region_3.4_spmd, %region_4.5_spmd} | conditional | bytes 11038812 | solution.py:1136
  68.0 20.1 %first.1 = (f32[56,64,256]{2,1,0:T(8,128)}, f32[56,256]{1,0:T(8,128)S(1)}, f32[56,256]{1,0:T(8,128)S(1)}, f32[54,64,256]{2,1,0:T(8,128)}, f32[54,64,256]{2,1,0:T...) custom-call(s32[6]{0:T(128)S(1)} %get-tuple-element.182.flags, f32[96,64,128]{2,1,0:T(8,128)S(1)} %get-tuple-element.183.refs_0_, ...), custom_call_target="tpu_custom_call" | custom-call | tf_op jit(solution)/shard_map/cond/branch_1_fun/first/pallas_call | solution.py:911
  90.2 6.6 %weights_second.1 = (bf16[3,768,256]{2,1,0:T(8,128)(2,1)}, bf16[3,768,256]{2,1,0:T(8,128)(2,1)}, bf16[3,768,256]{2,1,0:T(8,128)(2,1)}, bf16[3,768,256]{2,1,0:T(8...) custom-call(s32[6]{0:T(128)S(1)} %stack.84.flags, ...), custom_call_target="tpu_custom_call" | custom-call | tf_op jit(solution)/shard_map/weights_second/pallas_call | solution.py:911
  100.0 21.5 %second.1 = (f32[52,64,128]{2,1,0:T(8,128)}, f32[52,64,128]{2,1,0:T(8,128)}, f32[52,64,256]{2,1,0:T(8,128)}) custom-call(s32[6]{0:T(128)S(1)} %stack.84.flags, f32[54,64,256]{2,1,0:T(8,128)} %get-tuple-element.382.refs_0_, f32[54,256]{1,0:T(8,128)S(1)} %collective-permute-done.29.refs_1_, f32[118,256]{1,0:T(8,128)S(1)} %collective-permute-done.32.refs_2_, ...), custom_call_target="tpu_custom_call" | custom-call | tf_op jit(solution)/shard_map/second/pallas_call | solution.py:911
  123.0 20.8 %back_second.1 = (f32[52,64,256]{2,1,0:T(8,128)}, f32[52,64,256]{2,1,0:T(8,128)}, f32[114,256]{1,0:T(8,128)S(1)}, f32[50,256]{1,0:T(8,128)S(1)}) custom-call(s32[6]{0:T(128)S(1)} %stack.84.flags, f32[52,64,128]{2,1,0:T(8,128)} %get-tuple-element.369.refs_0_, f32[44,64,128]{2,1,0:T(8,128)} %collective-permute-done.30.refs_1_, ...), custom_call_target="tpu_custom_call" | custom-call | tf_op jit(solution)/shard_map/back_second/pallas_call | solution.py:911
  143.8 22.1 %conditional.9 = (f32[114,256]{1,0:T(8,128)}, f32[50,256]{1,0:T(8,128)}, f32[9,128,256]{2,1,0:T(8,128)}, f32[1,256]{1,0:T(1,128)}, f32[1152,256]{1,0:T(8,128)S(1)}) conditional(s32[]{:T(128)} %bitcast.5, () %tuple.85, (f32[114,256]{1,0:T(8,128)S(1)}, f32[50,256]{1,0:T(8,128)S(1)}, s32[6]{0:T(128)S(1)}, f32[54,64,256]{2,1,0:T(8,128)}, ...), branch_computations={%region_5.6_spmd, %region_6.7_spmd} | conditional | bytes 2528316 | solution.py:1136
  146.8 19.1 %weight_second.1 = (f32[9,128,256]{2,1,0:T(8,128)S(1)}, f32[9,128,256]{2,1,0:T(8,128)}, f32[1,256]{1,0:T(1,128)}) custom-call(s32[6]{0:T(128)S(1)} %get-tuple-element.192.flags, f32[54,64,256]{2,1,0:T(8,128)} %get-tuple-element.193.refs_0_, f32[54,256]{1,0:T(8,128)S(1)} %get-tuple-element.194.refs_1_, f32[118,256]{1,0:T(8,128)S(1)} %get-tuple-element.195.refs_2_, ...), custom_call_target="tpu_custom_call" | custom-call | tf_op jit(solution)/shard_map/cond/branch_1_fun/weight_second/pallas_call | solution.py:911
  165.9 24.7 %conditional.10 = (f32[10,128,256]{2,1,0:T(8,128)}, f32[1,256]{1,0:T(1,128)}, f32[1,256]{1,0:T(1,128)}, f32[50,64,256]{2,1,0:T(8,128)}, f32[1152,256]{1,0:T(8,128)}, /*index=5*/f32[1280,256]{1,0:T(8,128)}) conditional(s32[]{:T(128)} %bitcast.5, () %tuple.95, (s32[6]{0:T(128)S(1)}, f32[56,64,256]{2,1,0:T(8,128)}, f32[56,256]{1,0:T(8,128)S(1)}, ...), branch_computations={%region_7.8_spmd, %region_8.9_spmd} | conditional | bytes 7080008 | solution.py:1136
  166.0 24.6 %weight_first.1 = (f32[10,128,256]{2,1,0:T(8,128)}, f32[10,128,256]{2,1,0:T(8,128)}, f32[1,256]{1,0:T(1,128)}, f32[1,256]{1,0:T(1,128)}, f32[50,64,256]{2,1,0:T(8,128)}) custom-call(s32[6]{0:T(128)S(1)} %get-tuple-element.200.flags, f32[56,64,256]{2,1,0:T(8,128)} %get-tuple-element.201.refs_0_, f32[56,256]{1,0:T(8,128)S(1)} %get-tuple-element.202.refs_1_, ...), custom_call_target="tpu_custom_call" | custom-call | tf_op jit(solution)/shard_map/cond/branch_1_fun/weight_first/pallas_call | solution.py:911
  190.6 20.2 %conditional.11 = (f32[576,256]{1,0:T(8,128)S(1)}, f32[24,64,128]{2,1,0:T(8,128)S(1)}, f32[24,64,128]{2,1,0:T(8,128)}, f32[32,256]{1,0:T(8,128)}, f32[32,256]{1,...) conditional(s32[]{:T(128)} %bitcast.5, () %tuple.84, (s32[]{:T(128)}, f32[1152,256]{1,0:T(8,128)S(1)}, ...), branch_computations={%region_9.10_spmd, %region_10.11_spmd} | conditional | flops 442381 | bytes 16449974 | solution.py:1136
  193.4 15.2 %back_first_0.1 = (f32[24,64,128]{2,1,0:T(8,128)S(1)}, f32[24,64,128]{2,1,0:T(8,128)}, f32[32,256]{1,0:T(8,128)}, f32[32,256]{1,0:T(8,128)}, f32[64,256]{1,0:T(8,128)S(1)}) custom-call(s32[6]{0:T(128)} %copy-done.10, f32[50,64,256]{2,1,0:T(8,128)} %get-tuple-element.221.refs_0_, f32[52,64,128]{2,1,0:T(8,128)S(1)} %get-tuple-element.222.refs_1_, ...), custom_call_target="tpu_custom_call" | custom-call | tf_op jit(solution)/shard_map/cond/branch_1_fun/back_first_0/pallas_call | solution.py:911
  213.6 27.9 %conditional.12 = (f32[144,256]{1,0:T(8,128)S(1)}, f32[640,256]{1,0:T(8,128)}, f32[24,64,128]{2,1,0:T(8,128)S(1)}, f32[24,64,128]{2,1,0:T(8,128)}, f32[114,256]{1,0:T(8,128)}, /*index=5*/f32[50,256]{1,0:T(8,128)}) conditional(s32[]{:T(128)} %bitcast.5, () %tuple.83, (s32[]{:T(128)}, f32[576,256]{1,0:T(8,128)S(1)}, f32[1280,256]{1,0:T(8,128)}, ...), branch_computations={%region_11.12_spmd, %region_12.13_spmd} | conditional | flops 602153 | bytes 13222778 | solution.py:1136
  222.6 15.3 %back_first_1.1 = (f32[24,64,128]{2,1,0:T(8,128)S(1)}, f32[24,64,128]{2,1,0:T(8,128)}, f32[114,256]{1,0:T(8,128)}, f32[50,256]{1,0:T(8,128)}) custom-call(s32[6]{0:T(128)S(1)} %copy-done.11, f32[50,64,256]{2,1,0:T(8,128)} %get-tuple-element.240.refs_0_, f32[52,64,128]{2,1,0:T(8,128)S(1)} %get-tuple-element.241.refs_1_, ...), custom_call_target="tpu_custom_call" | custom-call | tf_op jit(solution)/shard_map/cond/branch_1_fun/back_first_1/pallas_call | solution.py:911
  241.6 21.1 %conditional.13 = (f32[114,256]{1,0:T(8,128)}, f32[50,256]{1,0:T(8,128)}, f32[160,256]{1,0:T(8,128)S(1)}, f32[144,128]{1,0:T(8,128)S(1)}, f32[96,64,128]{2,1,0:T(8,128)}) conditional(s32[]{:T(128)} %bitcast.5, () %tuple.82, (f32[114,256]{1,0:T(8,128)}, f32[50,256]{1,0:T(8,128)}, s32[]{:T(128)}, f32[640,256]{1,0:T(8,128)}, ...), branch_computations={%region_13.14_spmd, %region_14.15_spmd} | conditional | flops 141340 | bytes 5104220 | solution.py:1136
  255.3 6.4 %collective-permute-done.12 = f32[160,256]{1,0:T(8,128)S(1)} collective-permute-done((f32[160,256]{1,0:T(8,128)S(1)}, f32[160,256]{1,0:T(8,128)S(1)}, u32[]{:S(2)}, u32[]{:S(2)}) %collective-permute-start.12) | collective-permute-done | bytes 163872 | tf_op jit(solution)/shard_map/cond/branch_1_fun/ppermute | solution.py:990
  265.8 3.7 %multiply_reduce_fusion.2 = (f32[128]{0:T(128)S(1)}, f32[128]{0:T(128)S(1)}, f32[128]{0:T(128)S(1)}, f32[128]{0:T(128)S(1)}) fusion(f32[56,64,256]{2,1,0:T(8,128)} %get-tuple-element.391.refs_6_, f32[64,128]{1,0:T(8,128)S(1)} %get-tuple-element.494, pred[48]{0:T(512)(128)(4,1)S(1)} %compare_and_fusion, f32[48,128]{1,0:T(8,128)S(1)} %get-tuple-element.496, ...), kind=kLoop, calls=%fused_computation.46 | loop fusion | flops 8650240 | bytes 6469808 | tf_op jit(solution)/shard_map/reduce_sum | solution.py:1308
  297.1 6.1 %collective-permute-done.51 = f32[640,128]{1,0:T(8,128)S(1)} collective-permute-done((f32[640,128]{1,0:T(8,128)S(1)}, f32[640,128]{1,0:T(8,128)S(1)}, u32[]{:S(2)}, u32[]{:S(2)}) %collective-permute-start.51) | collective-permute-done | bytes 327712 | tf_op jit(solution)/shard_map/ppermute | solution.py:996
  308.4 3.7 %final_own.1.rest_0_ = f32[96,64,128]{2,1,0:T(8,128)} custom-call(s32[6]{0:T(128)S(1)} %copy-done.9, f32[96,64,128]{2,1,0:T(8,128)S(1)} %copy-done.3, f32[24,64,128]{2,1,0:T(8,128)S(1)} %get-tuple-element.441.lower_upper, f32[24,64,128]{2,1,0:T(8,128)} %copy-done.4, f32[164,128]{1,0:T(8,128)} %get-tuple-element.489.rims, f32[8,128]{1,0:T(8,128)S(1)} %copy-done.20, ...), custom_call_target="tpu_custom_call" | custom-call | bytes 9437184 | tf_op jit(solution)/shard_map/final_own/pallas_call | solution.py:787
  312.8 3.9 %final_got.1 = f32[96,64,128]{2,1,0:T(8,128)} custom-call(s32[6]{0:T(128)S(1)} %copy-done.9, f32[96,64,128]{2,1,0:T(8,128)S(1)} %copy-done.3, f32[24,64,128]{2,1,0:T(8,128)} %collective-permute-done.34.lower_upper, f32[24,64,128]{2,1,0:T(8,128)} %copy-done.7, f32[164,128]{1,0:T(8,128)} %copy-done.16, ...), custom_call_target="tpu_custom_call", output_to_operand_aliasing={{}: (7, {})} | custom-call | bytes 9437184 | tf_op jit(solution)/shard_map/final_got/pallas_call | solution.py:787
  (242 shorter events, 125.1 us)
Async XLA Ops:
  3.8 13.2 %collective-permute-start.26 = (f32[616,128]{1,0:T(8,128)}, f32[616,128]{1,0:T(8,128)S(1)}, u32[]{:S(2)}, u32[]{:S(2)}) collective-permute-start(f32[616,128]{1,0:T(8,128)} %pad_maximum_fusion.6), channel_id=1, source_target_pairs={{0,1},{1,0},{2,3},{3,2},{4,5},{5,4},{6,7},{7,6},{8,9},{9,8},{10,11... | collective-permute-start | bytes 946184 | tf_op jit(solution)/shard_map/ppermute | solution.py:951
  17.1 48.1 %collective-permute-start.28 = (f32[52,64,128]{2,1,0:T(8,128)}, f32[52,64,128]{2,1,0:T(8,128)}, u32[]{:S(2)}, u32[]{:S(2)}) collective-permute-start(f32[52,64,128]{2,1,0:T(8,128)} %get-tuple-element.372), channel_id=1, source_target_pairs={{0,1},{1,0},{2,3},{3,2},{4,5},{5,4},{6,7},{7,6},{8,9},{9,8},{10,11... | collective-permute-start | bytes 5111816 | tf_op jit(solution)/shard_map/ppermute | solution.py:951
  26.8 12.6 %collective-permute-start.19 = (f32[616,128]{1,0:T(8,128)S(1)}, f32[616,128]{1,0:T(8,128)}, u32[]{:S(2)}, u32[]{:S(2)}) collective-permute-start(f32[616,128]{1,0:T(8,128)S(1)} %get-tuple-element.528.refs_1_), channel_id=1, source_target_pairs={{0,8},{2,10},{4,12},{6,14},{8,0},{10,2},{12,4},{14,6},{16,24},{18,... | collective-permute-start | bytes 946184 | tf_op jit(solution)/shard_map/cond/branch_1_fun/ppermute | solution.py:954
  41.3 14.0 %collective-permute-start.23 = (f32[1232,128]{1,0:T(8,128)}, f32[1232,128]{1,0:T(8,128)}, u32[]{:S(2)}, u32[]{:S(2)}) collective-permute-start(f32[1232,128]{1,0:T(8,128)} %pad_maximum_fusion.1), channel_id=1, source_target_pairs={{0,4},{2,6},{4,0},{6,2},{8,12},{10,14},{12,8},{14,10},{16,20},{18,... | collective-permute-start | bytes 1892360 | tf_op jit(solution)/shard_map/cond/branch_1_fun/ppermute | solution.py:954
  65.2 34.8 %collective-permute-start.30 = (f32[44,64,128]{2,1,0:T(8,128)}, f32[44,64,128]{2,1,0:T(8,128)}, u32[]{:S(2)}, u32[]{:S(2)}) collective-permute-start(f32[44,64,128]{2,1,0:T(8,128)} %get-tuple-element.379), channel_id=1, source_target_pairs={{0,1},{1,0},{2,3},{3,2},{4,5},{5,4},{6,7},{7,6},{8,9},{9,8},{10,11... | collective-permute-start | bytes 4325384 | tf_op jit(solution)/shard_map/ppermute | solution.py:951
  66.6 54.9 %collective-permute-start.31 = (f32[8,64,128]{2,1,0:T(8,128)}, f32[8,64,128]{2,1,0:T(8,128)}, u32[]{:S(2)}, u32[]{:S(2)}) collective-permute-start(f32[8,64,128]{2,1,0:T(8,128)} %get-tuple-element.381), channel_id=1, source_target_pairs={{0,1},{1,0},{2,3},{3,2},{4,5},{5,4},{6,7},{7,6},{8,9},{9,8},{10,11... | collective-permute-start | bytes 786440 | tf_op jit(solution)/shard_map/ppermute | solution.py:951
  121.5 44.3 %collective-permute-start.33 = (f32[52,64,128]{2,1,0:T(8,128)}, f32[52,64,128]{2,1,0:T(8,128)}, u32[]{:S(2)}, u32[]{:S(2)}) collective-permute-start(f32[52,64,128]{2,1,0:T(8,128)} %get-tuple-element.408), channel_id=1, source_target_pairs={{0,1},{1,0},{2,3},{3,2},{4,5},{5,4},{6,7},{7,6},{8,9},{9,8},{10,11... | collective-permute-start | bytes 5111816 | tf_op jit(solution)/shard_map/ppermute | solution.py:951
  143.8 22.1 %collective-permute-start = (f32[114,256]{1,0:T(8,128)S(1)}, f32[114,256]{1,0:T(8,128)}, u32[]{:S(2)}, u32[]{:S(2)}) collective-permute-start(f32[114,256]{1,0:T(8,128)S(1)} %get-tuple-element.190), channel_id=1, source_target_pairs={{0,4},{2,6},{4,8},{6,10},{8,12},{10,14},{12,0},{14,2},{16,20},{18,... | collective-permute-start | bytes 350216 | tf_op jit(solution)/shard_map/cond/branch_1_fun/ppermute | solution.py:945
  144.1 21.7 %collective-permute-start.1 = (f32[50,256]{1,0:T(8,128)S(1)}, f32[50,256]{1,0:T(8,128)}, u32[]{:S(2)}, u32[]{:S(2)}) collective-permute-start(f32[50,256]{1,0:T(8,128)S(1)} %get-tuple-element.191), channel_id=1, source_target_pairs={{0,12},{2,14},{4,0},{6,2},{8,4},{10,6},{12,8},{14,10},{16,28},{18,... | collective-permute-start | bytes 153608 | tf_op jit(solution)/shard_map/cond/branch_1_fun/ppermute | solution.py:948
  165.9 24.7 %collective-permute-start.2 = (f32[9,128,256]{2,1,0:T(8,128)}, f32[9,128,256]{2,1,0:T(8,128)}, u32[]{:S(2)}, u32[]{:S(2)}) collective-permute-start(f32[9,128,256]{2,1,0:T(8,128)} %get-tuple-element.215), channel_id=1, source_target_pairs={{0,2},{2,0},{4,6},{6,4},{8,10},{10,8},{12,14},{14,12},{16,18},{18,... | collective-permute-start | bytes 3538952 | tf_op jit(solution)/shard_map/cond/branch_1_fun/ppermute | solution.py:954
  190.9 19.9 %collective-permute-start.4 = (f32[10,128,256]{2,1,0:T(8,128)}, f32[10,128,256]{2,1,0:T(8,128)}, u32[]{:S(2)}, u32[]{:S(2)}) collective-permute-start(f32[10,128,256]{2,1,0:T(8,128)} %get-tuple-element.234), channel_id=1, source_target_pairs={{0,2},{2,0},{4,6},{6,4},{8,10},{10,8},{12,14},{14,12},{16,18},{18,... | collective-permute-start | bytes 3932168 | tf_op jit(solution)/shard_map/cond/branch_1_fun/ppermute | solution.py:954
  193.4 15.9 %collective-permute-start.3 = (f32[576,256]{1,0:T(8,128)}, f32[576,256]{1,0:T(8,128)}, u32[]{:S(2)}, u32[]{:S(2)}) collective-permute-start(f32[576,256]{1,0:T(8,128)} %dynamic-slice_add_fusion), channel_id=1, source_target_pairs={{0,4},{2,6},{4,0},{6,2},{8,12},{10,14},{12,8},{14,10},{16,20},{18,... | collective-permute-start | bytes 1769480 | tf_op jit(solution)/shard_map/cond/branch_1_fun/ppermute | solution.py:990
  210.9 30.7 %collective-permute-start.34 = (f32[24,64,128]{2,1,0:T(8,128)}, f32[24,64,128]{2,1,0:T(8,128)}, u32[]{:S(2)}, u32[]{:S(2)}) collective-permute-start(f32[24,64,128]{2,1,0:T(8,128)} %get-tuple-element.428), channel_id=1, source_target_pairs={{0,1},{1,0},{2,3},{3,2},{4,5},{5,4},{6,7},{7,6},{8,9},{9,8},{10,11... | collective-permute-start | bytes 2359304 | tf_op jit(solution)/shard_map/ppermute | solution.py:951
  216.1 23.0 %collective-permute-start.8 = (f32[640,256]{1,0:T(8,128)}, f32[640,256]{1,0:T(8,128)}, u32[]{:S(2)}, u32[]{:S(2)}) collective-permute-start(f32[640,256]{1,0:T(8,128)} %dynamic-slice_add_fusion.1), channel_id=1, source_target_pairs={{0,4},{2,6},{4,0},{6,2},{8,12},{10,14},{12,8},{14,10},{16,20},{18,... | collective-permute-start | bytes 1966088 | tf_op jit(solution)/shard_map/cond/branch_1_fun/ppermute | solution.py:990
  218.2 19.7 %collective-permute-start.7 = (f32[144,256]{1,0:T(8,128)}, f32[144,256]{1,0:T(8,128)}, u32[]{:S(2)}, u32[]{:S(2)}) collective-permute-start(f32[144,256]{1,0:T(8,128)} %get-tuple-element.461), channel_id=1, source_target_pairs={{0,24},{2,26},{4,28},{6,30},{8,16},{10,18},{12,20},{14,22},{16,8},... | collective-permute-start | bytes 442376 | tf_op jit(solution)/shard_map/cond/branch_1_fun/ppermute | solution.py:990
  219.6 18.4 %collective-permute-start.6 = (f32[144,256]{1,0:T(8,128)}, f32[144,256]{1,0:T(8,128)}, u32[]{:S(2)}, u32[]{:S(2)}) collective-permute-start(f32[144,256]{1,0:T(8,128)} %get-tuple-element.462), channel_id=1, source_target_pairs={{0,16},{2,18},{4,20},{6,22},{8,24},{10,26},{12,28},{14,30},{16,0},... | collective-permute-start | bytes 442376 | tf_op jit(solution)/shard_map/cond/branch_1_fun/ppermute | solution.py:990
  220.2 17.7 %collective-permute-start.5 = (f32[144,256]{1,0:T(8,128)}, f32[144,256]{1,0:T(8,128)}, u32[]{:S(2)}, u32[]{:S(2)}) collective-permute-start(f32[144,256]{1,0:T(8,128)} %get-tuple-element.460), channel_id=1, source_target_pairs={{0,8},{2,10},{4,12},{6,14},{8,0},{10,2},{12,4},{14,6},{16,24},{18,... | collective-permute-start | bytes 442376 | tf_op jit(solution)/shard_map/cond/branch_1_fun/ppermute | solution.py:990
  241.6 21.0 %collective-permute-start.9 = (f32[114,256]{1,0:T(8,128)}, f32[114,256]{1,0:T(8,128)}, u32[]{:S(2)}, u32[]{:S(2)}) collective-permute-start(f32[114,256]{1,0:T(8,128)} %get-tuple-element.255), channel_id=1, source_target_pairs={{0,4},{2,6},{4,8},{6,10},{8,12},{10,14},{12,0},{14,2},{16,20},{18,... | collective-permute-start | bytes 350216 | tf_op jit(solution)/shard_map/cond/branch_1_fun/ppermute | solution.py:945
  242.3 20.3 %collective-permute-start.10 = (f32[50,256]{1,0:T(8,128)}, f32[50,256]{1,0:T(8,128)}, u32[]{:S(2)}, u32[]{:S(2)}) collective-permute-start(f32[50,256]{1,0:T(8,128)} %get-tuple-element.256), channel_id=1, source_target_pairs={{0,12},{2,14},{4,0},{6,2},{8,4},{10,6},{12,8},{14,10},{16,28},{18,... | collective-permute-start | bytes 153608 | tf_op jit(solution)/shard_map/cond/branch_1_fun/ppermute | solution.py:948
  248.5 13.2 %collective-permute-start.12 = (f32[160,256]{1,0:T(8,128)S(1)}, f32[160,256]{1,0:T(8,128)S(1)}, u32[]{:S(2)}, u32[]{:S(2)}) collective-permute-start(f32[160,256]{1,0:T(8,128)S(1)} %get-tuple-element.465), channel_id=1, source_target_pairs={{0,16},{2,18},{4,20},{6,22},{8,24},{10,26},{12,28},{14,30},{16,0},... | collective-permute-start | bytes 491528 | tf_op jit(solution)/shard_map/cond/branch_1_fun/ppermute | solution.py:990
  262.6 17.7 %collective-permute-start.35 = (f32[24,64,128]{2,1,0:T(8,128)}, f32[24,64,128]{2,1,0:T(8,128)S(1)}, u32[]{:S(2)}, u32[]{:S(2)}) collective-permute-start(f32[24,64,128]{2,1,0:T(8,128)} %get-tuple-element.434), channel_id=1, source_target_pairs={{0,1},{1,0},{2,3},{3,2},{4,5},{5,4},{6,7},{7,6},{8,9},{9,8},{10,11... | collective-permute-start | bytes 2359304 | tf_op jit(solution)/shard_map/ppermute | solution.py:951
  281.1 23.1 %collective-permute-start.40 = (f32[8,256]{1,0:T(8,128)S(1)}, f32[8,256]{1,0:T(8,128)S(1)}, u32[]{:S(2)}, u32[]{:S(2)}) collective-permute-start(f32[8,256]{1,0:T(8,128)S(1)} %select_add_fusion.1), channel_id=1, source_target_pairs={{0,16},{2,18},{4,20},{6,22},{8,24},{10,26},{12,28},{14,30},{16,0},... | collective-permute-start | bytes 24584 | tf_op jit(solution)/shard_map/ppermute | solution.py:954
  297.1 19.6 %collective-permute-start.46 = (f32[9,128,128]{2,1,0:T(8,128)}, f32[9,128,128]{2,1,0:T(8,128)}, u32[]{:S(2)}, u32[]{:S(2)}) collective-permute-start(f32[9,128,128]{2,1,0:T(8,128)} %bitcast.24.second_mine), channel_id=1, source_target_pairs={{0,2},{2,0},{4,6},{6,4},{8,10},{10,8},{12,14},{14,12},{16,18},{18,... | collective-permute-start | bytes 1769480 | tf_op jit(solution)/shard_map/ppermute | solution.py:954
  304.1 12.6 %collective-permute-start.52 = (f32[10,128,128]{2,1,0:T(8,128)}, f32[10,128,128]{2,1,0:T(8,128)}, u32[]{:S(2)}, u32[]{:S(2)}) collective-permute-start(f32[10,128,128]{2,1,0:T(8,128)} %bitcast.25.first_mine), channel_id=1, source_target_pairs={{0,2},{2,0},{4,6},{6,4},{8,10},{10,8},{12,14},{14,12},{16,18},{18,... | collective-permute-start | bytes 1966088 | tf_op jit(solution)/shard_map/ppermute | solution.py:954
  (61 other events, 706.3 us)
